TPU v7x, 128 devices: a whole 4x4x4 slice. The times are simulated.
128 devices in a mesh: leaf: 8 (over x, core), panel: 16 (over z, y).
Axes of the slice: x: 4, y: 4, z: 4, core: 2. Of those that a mesh axis runs over, the one named last changes fastest.
Arguments:
- leaf_source: float32 [32, 16384], P(None, ('leaf', 'panel')), may hold values from -6 to 6
- leaf_noise: float32 [32, 16384], P(None, ('leaf', 'panel')), may hold values from -6 to 6
- sep_source: float32 [32, 16384], P(None, ('leaf', 'panel')), may hold values from -6 to 6
- sep_noise: float32 [32, 16384], P(None, ('leaf', 'panel')), may hold values from -6 to 6
- leaf_inverse: bfloat16 [8, 2048, 2048], P('leaf', 'panel'), may hold values from -0.125 to 0.125
- leaf_coupling: bfloat16 [8, 2048, 2048], P('leaf', 'panel'), may hold values from -0.0625 to 0.0625
- sep_inverse: bfloat16 [8, 2048, 2048], P('leaf', 'panel'), may hold values from -0.125 to 0.125
- sep_coupling: bfloat16 [8, 2048, 2048], P('leaf', 'panel'), may hold values from -0.0625 to 0.0625
- sep_length: int32 [8], P('leaf'), may hold values from 1024 to 2048, as said below
- leaf_map: int32 [8, 2048], P('leaf'), may hold values from 0 to 2047
- sep_map: int32 [8, 2048], P('leaf'), may hold values from 0 to 2047
Outputs:
- leaf_sample: float32 [32, 16384], P(None, ('leaf', 'panel'))
- sep_sample: float32 [32, 16384], P(None, ('leaf', 'panel'))
Inputs may be any that keep to these rules, and one draw needn't show every extreme that they name: `sep_length`: some front has all 2048 rows live and another exactly half of them.
All inputs are finite; a program needn't handle non-finite values.
Results may differ from a plain program's by a relative error of at most 0.012.
Values may be sent and summed in bfloat16 or wider, within the bound.
A program may use at most 64 MiB of HBM per device.

v0:
```python
import jax
import jax.numpy as jnp
from jax import lax
from jax.sharding import PartitionSpec as P

LEVELS = 4


def shifted(value, axis, steps):
    count = lax.axis_size(axis)
    initial, last = (max(0, -steps), min(count, count - steps))
    return lax.ppermute(value, axis, [(source, source + steps) for source in range(initial, last)])


def spread(values, targets, sep_width):
    blank_sum = jnp.zeros((values.shape[0], sep_width), jnp.float32)
    return blank_sum.at[:, targets].add(values)


def lifted(mapped):
    summed = lax.psum(mapped, "panel")
    return summed


def own_share(arriving, share_rows, panel_index):
    picked = lax.dynamic_slice_in_dim(arriving, panel_index * share_rows, share_rows, 1)
    return picked


def publish(sample_rows):
    outgoing = lax.all_gather(sample_rows, "panel", axis=1, tiled=True)
    return outgoing


def climb(summed, offset):
    return shifted(summed, "leaf", offset)


def descend(sending, offset):
    return shifted(sending, "leaf", offset)


def shards(
    leaf_source,
    leaf_noise,
    sep_source,
    sep_noise,
    leaf_inverse,
    leaf_coupling,
    sep_inverse,
    sep_coupling,
    sep_length,
    leaf_map,
    sep_map,
):
    member = lax.axis_index("leaf")
    panel_index = lax.axis_index("panel")
    share_rows = sep_source.shape[1]
    sep_width = sep_coupling.shape[2]
    samples_here = sep_source.shape[0]
    number = member + 1
    my_level = 1 + sum(
        [(number % (1 << bit_index) == 0).astype(jnp.int32) for bit_index in range(1, LEVELS)]
    )
    stride = jnp.left_shift(jnp.int32(1), my_level - 1)
    left_child = jnp.logical_or(number // stride % 4 == 1, my_level == LEVELS - 1)
    row_index = panel_index * share_rows + jnp.arange(share_rows, dtype=jnp.int32)
    active = (row_index < sep_length[0]).astype(jnp.float32)[None, :]
    inverse = sep_inverse[0]
    coupling = sep_coupling[0]
    zero_full = jnp.zeros((samples_here, sep_width), jnp.float32)
    zero_share = jnp.zeros_like(sep_source)
    leaf_partial = jnp.dot(
        leaf_source.astype(jnp.bfloat16), leaf_inverse[0], preferred_element_type=jnp.float32
    )
    leaf_solved = lax.psum_scatter(leaf_partial, "panel", scatter_dimension=1, tiled=True)
    leaf_update = jnp.dot(
        leaf_solved.astype(jnp.bfloat16), leaf_coupling[0], preferred_element_type=jnp.float32
    )
    leaf_summed = lifted(spread(leaf_update, leaf_map[0], sep_width))
    neighbour = shifted(leaf_summed, "leaf", -1)
    pending = own_share(
        jnp.where(my_level == 1, leaf_summed + neighbour, 0.0), share_rows, panel_index
    )
    solved = zero_share
    for section in range(1, LEVELS + 1):
        working = my_level == section
        right_side = (active * (sep_source - pending)).astype(jnp.bfloat16)
        partial_value = lax.cond(
            working,
            lambda: jnp.dot(right_side, inverse, preferred_element_type=jnp.float32),
            lambda: zero_full,
        )
        solved_now = lax.psum_scatter(partial_value, "panel", scatter_dimension=1, tiled=True)
        solved = jnp.where(working, active * solved_now, solved)
        if section < LEVELS:
            offset = 1 << section - 1
            solved_half = solved.astype(jnp.bfloat16)
            update = lax.cond(
                working,
                lambda: spread(
                    jnp.dot(solved_half, coupling, preferred_element_type=jnp.float32),
                    sep_map[0],
                    sep_width,
                ),
                lambda: zero_full,
            )
            summed = lifted(update)
            arriving = climb(summed, offset)
            if section < LEVELS - 1:
                arriving = arriving + climb(summed, -offset)
            pending = pending + jnp.where(
                my_level == section + 1, own_share(arriving, share_rows, panel_index), 0.0
            )
    sample = zero_share
    parent_view = jnp.zeros((samples_here, sep_width), jnp.bfloat16)
    sending = publish(sample.astype(jnp.bfloat16))
    for section in range(LEVELS, 0, -1):
        working = my_level == section
        if section < LEVELS:
            correction = lax.cond(
                working,
                lambda: jnp.dot(parent_view, coupling.T, preferred_element_type=jnp.float32),
                lambda: zero_share,
            )
        else:
            correction = zero_share
        residual = (active * (solved + sep_noise - correction)).astype(jnp.bfloat16)
        whole_residual = lax.all_gather(residual, "panel", axis=1, tiled=True)
        result = lax.cond(
            working,
            lambda: active * jnp.dot(whole_residual, inverse.T, preferred_element_type=jnp.float32),
            lambda: zero_share,
        )
        sample = jnp.where(working, result, sample)
        sending = publish(sample.astype(jnp.bfloat16))
        if section > 1:
            offset = 1 << section - 2
            arrived = descend(sending, -offset)
            if section < LEVELS:
                lower_parent = descend(sending, offset)
                arrived = jnp.where(left_child, arrived, lower_parent)
            parent_view = jnp.take(arrived, sep_map[0], axis=1)
    lower_parent = shifted(sending, "leaf", 1)
    parent_rows = jnp.where(my_level == 1, sending, lower_parent)
    mapped_back = jnp.take(parent_rows, leaf_map[0], axis=1)
    leaf_correction = jnp.dot(mapped_back, leaf_coupling[0].T, preferred_element_type=jnp.float32)
    leaf_residual = (leaf_solved + leaf_noise - leaf_correction).astype(jnp.bfloat16)
    whole_leaf = lax.all_gather(leaf_residual, "panel", axis=1, tiled=True)
    leaf_sample = jnp.dot(whole_leaf, leaf_inverse[0].T, preferred_element_type=jnp.float32)
    return (leaf_sample, sample)


def solution(mesh):
    in_specs = (
        P(None, ("leaf", "panel")),
        P(None, ("leaf", "panel")),
        P(None, ("leaf", "panel")),
        P(None, ("leaf", "panel")),
        P("leaf", "panel", None),
        P("leaf", "panel", None),
        P("leaf", "panel", None),
        P("leaf", "panel", None),
        P("leaf"),
        P("leaf", None),
        P("leaf", None),
    )
    out_specs = (P(None, ("leaf", "panel")), P(None, ("leaf", "panel")))
    return jax.shard_map(shards, mesh=mesh, in_specs=in_specs, out_specs=out_specs, check_vma=False)
```

profile of v0, /device:TPU:1, one launch (start us, length us, event | category | flops | bytes accessed | tf_op | source)
XLA Modules:
  0.0 1068.6 jit_solution(14725766131365702129)
XLA Ops:
  7.2 2.0 fusion.14
  9.9 74.9 %reduce-scatter.6.cloned.1.call-done = f32[32,128]{1,0:T(8,128)} async-done(((f32[32,2048]{1,0:T(8,128)}), f32[32,128]{1,0:T(8,128)}) %reduce-scatter.6.cloned.1.call-update) | async-done | bytes 16400 | tf_op jit(solution)/shard_map/reduce_scatter | solution.py:76
  86.1 11.7 %scatter_custom_fusion.3 = f32[32,2048]{0,1:T(8,128)S(1)} fusion(s32[2048]{0:T(1024)S(1)} %bitcast.95, f32[2048,32]{1,0:T(8,128)S(1)} %copy.132, f32[]{:T(128)} %constant.120.clone.1), kind=kCustom, calls=%fused_computation.24 | custom fusion | flops 65536 | bytes 262148 | tf_op jit(solution)/shard_map/scatter-add | solution.py:17
  99.0 84.1 %all-reduce.5.cloned.1.call-done = f32[32,2048]{1,0:T(8,128)} async-done(((f32[32,2048]{1,0:T(8,128)}), f32[32,2048]{1,0:T(8,128)}) %all-reduce.5.cloned.1.call-update) | async-done | bytes 262160 | tf_op jit(solution)/shard_map/psum | solution.py:21
  183.0 3.9 collective-permute-start
  187.6 4.6 collective-permute-done
  193.8 69.0 %reduce-scatter.8.cloned.1.call-done = f32[32,128]{1,0:T(8,128)} async-done(((f32[32,2048]{1,0:T(8,128)}), f32[32,128]{1,0:T(8,128)}) %reduce-scatter.8.cloned.1.call-update) | async-done | bytes 16400 | tf_op jit(solution)/shard_map/reduce_scatter | solution.py:94
  264.8 97.5 %all-reduce.7.cloned.1.call-done = f32[32,2048]{1,0:T(8,128)} async-done(((f32[32,2048]{1,0:T(8,128)}), f32[32,2048]{1,0:T(8,128)}) %all-reduce.7.cloned.1.call-update) | async-done | bytes 262160 | tf_op jit(solution)/shard_map/psum | solution.py:21
  362.2 4.9 collective-permute-start.1
  367.2 1.9 collective-permute-start.2
  369.1 1.7 collective-permute-done.1
  370.8 4.3 collective-permute-done.2
  376.8 69.0 %reduce-scatter.10.cloned.1.call-done = f32[32,128]{1,0:T(8,128)} async-done(((f32[32,2048]{1,0:T(8,128)}), f32[32,128]{1,0:T(8,128)}) %reduce-scatter.10.cloned.1.call-update) | async-done | bytes 16400 | tf_op jit(solution)/shard_map/reduce_scatter | solution.py:94
  446.5 13.4 %conditional.17 = (f32[32,2048]{0,1:T(8,128)S(1)}) conditional(s32[]{:T(128)} %convert_element_type.109, () %tuple.99, (s32[1,2048]{1,0:T(1,128)S(1)}, bf16[32,128]{1,0:T(8,128)(2,1)S(1)}, bf16[128,2048]{1,0:T(8,128)(2,1)S(1)}) %tuple.237), branch_computations={%region_13.14_spmd, %region_14.16_spmd} | conditional | flops 16848896 | bytes 1073672 | solution.py:99
  446.5 1.3 fusion.45
  447.9 12.1 %scatter_custom_fusion.1 = f32[32,2048]{0,1:T(8,128)S(1)} fusion(s32[2048]{0:T(1024)S(1)} %bitcast.97, f32[2048,32]{1,0:T(8,128)} %fusion.45, f32[]{:T(128)} %constant.61.clone), kind=kCustom, calls=%fused_computation.15 | custom fusion | flops 65536 | bytes 262656 | tf_op jit(solution)/shard_map/cond/branch_1_fun/scatter-add | solution.py:17
  461.1 81.7 %all-reduce.9.cloned.1.call-done = f32[32,2048]{1,0:T(8,128)} async-done(((f32[32,2048]{1,0:T(8,128)}), f32[32,2048]{1,0:T(8,128)}) %all-reduce.9.cloned.1.call-update) | async-done | bytes 262160 | tf_op jit(solution)/shard_map/psum | solution.py:21
  542.7 3.1 collective-permute-start.3
  545.8 1.3 collective-permute-start.4
  547.1 2.6 collective-permute-done.3
  549.7 3.7 collective-permute-done.4
  554.3 71.9 %reduce-scatter.12.cloned.1.call-done = f32[32,128]{1,0:T(8,128)} async-done(((f32[32,2048]{1,0:T(8,128)}), f32[32,128]{1,0:T(8,128)}) %reduce-scatter.12.cloned.1.call-update) | async-done | bytes 16400 | tf_op jit(solution)/shard_map/reduce_scatter | solution.py:94
  628.1 93.5 %all-reduce.11.cloned.1.call-done = f32[32,2048]{1,0:T(8,128)} async-done(((f32[32,2048]{1,0:T(8,128)}), f32[32,2048]{1,0:T(8,128)}) %all-reduce.11.cloned.1.call-update) | async-done | bytes 262160 | tf_op jit(solution)/shard_map/psum | solution.py:21
  721.6 4.8 collective-permute-start.5
  726.4 3.7 collective-permute-done.5
  730.9 72.6 %reduce-scatter.14.cloned.1.call-done = f32[32,128]{1,0:T(8,128)} async-done(((f32[32,2048]{1,0:T(8,128)}), f32[32,128]{1,0:T(8,128)}) %reduce-scatter.14.cloned.1.call-update) | async-done | bytes 16400 | tf_op jit(solution)/shard_map/reduce_scatter | solution.py:94
  804.3 16.9 %all_gather.27 = bf16[32,2048]{1,0:T(8,128)(2,1)S(1)} all-gather(bf16[32,128]{1,0:T(8,128)(2,1)S(1)} %get-tuple-element.271), channel_id=1, replica_groups=mesh['leaf'=8,'panel'=16] {'panel'}, dimensions={1}, use_global_device_ids=true | all-gather | bytes 139264 | tf_op jit(solution)/shard_map/all_gather | solution.py:129
  821.2 16.5 %all_gather.28 = bf16[32,2048]{1,0:T(8,128)(2,1)S(1)} all-gather(bf16[32,128]{1,0:T(8,128)(2,1)S(1)} %select_convert_fusion), channel_id=1, replica_groups=mesh['leaf'=8,'panel'=16] {'panel'}, dimensions={1}, use_global_device_ids=true | all-gather | bytes 139264 | tf_op jit(solution)/shard_map/all_gather | solution.py:31
  839.0 5.9 collective-permute-done.6
  845.2 6.2 gather_fusion
  851.8 16.9 %all_gather.29 = bf16[32,2048]{1,0:T(8,128)(2,1)S(1)} all-gather(bf16[32,128]{1,0:T(8,128)(2,1)S(1)} %multiply_convert_fusion.2), channel_id=1, replica_groups=mesh['leaf'=8,'panel'=16] {'panel'}, dimensions={1}, use_global_device_ids=true | all-gather | bytes 139264 | tf_op jit(solution)/shard_map/all_gather | solution.py:129
  868.6 16.8 %all_gather.30 = bf16[32,2048]{1,0:T(8,128)(2,1)S(1)} all-gather(bf16[32,128]{1,0:T(8,128)(2,1)S(1)} %get-tuple-element.269), channel_id=1, replica_groups=mesh['leaf'=8,'panel'=16] {'panel'}, dimensions={1}, use_global_device_ids=true | all-gather | bytes 139264 | tf_op jit(solution)/shard_map/all_gather | solution.py:31
  885.5 1.3 collective-permute-start.7
  886.8 4.4 collective-permute-start.8
  891.6 1.5 collective-permute-done.8
  893.4 6.2 gather_fusion.1
  900.2 16.9 %all_gather.31 = bf16[32,2048]{1,0:T(8,128)(2,1)S(1)} all-gather(bf16[32,128]{1,0:T(8,128)(2,1)S(1)} %multiply_convert_fusion.1), channel_id=1, replica_groups=mesh['leaf'=8,'panel'=16] {'panel'}, dimensions={1}, use_global_device_ids=true | all-gather | bytes 139264 | tf_op jit(solution)/shard_map/all_gather | solution.py:129
  917.5 16.5 %all_gather.32 = bf16[32,2048]{1,0:T(8,128)(2,1)S(1)} all-gather(bf16[32,128]{1,0:T(8,128)(2,1)S(1)} %fusion.27), channel_id=1, replica_groups=mesh['leaf'=8,'panel'=16] {'panel'}, dimensions={1}, use_global_device_ids=true | all-gather | bytes 139264 | tf_op jit(solution)/shard_map/all_gather | solution.py:31
  933.9 40.2 %collective-permute-start.10 = (bf16[32,2048]{1,0:T(8,128)(2,1)S(1)}, bf16[32,2048]{1,0:T(8,128)(2,1)S(1)}, u32[]{:S(2)}, u32[]{:S(2)}) collective-permute-start(bf16[32,2048]{1,0:T(8,128)(2,1)S(1)} %all_gather.32), channel_id=1, source_target_pairs={{0,16},{16,32},{32,48},{48,64},{64,80},{80,96},{96,112},{1,17},{17... | collective-permute-start | bytes 393224 | tf_op jit(solution)/shard_map/ppermute | solution.py:12
  974.2 1.9 collective-permute-start.9
  976.1 4.3 collective-permute-done.9
  980.8 6.2 gather_fusion.2
  987.3 17.5 %all_gather.33 = bf16[32,2048]{1,0:T(8,128)(2,1)S(1)} all-gather(bf16[32,128]{1,0:T(8,128)(2,1)S(1)} %multiply_convert_fusion), channel_id=1, replica_groups=mesh['leaf'=8,'panel'=16] {'panel'}, dimensions={1}, use_global_device_ids=true | all-gather | bytes 139264 | tf_op jit(solution)/shard_map/all_gather | solution.py:129
  1005.4 16.1 %all_gather.34 = bf16[32,2048]{1,0:T(8,128)(2,1)S(1)} all-gather(bf16[32,128]{1,0:T(8,128)(2,1)S(1)} %get-tuple-element.267), channel_id=1, replica_groups=mesh['leaf'=8,'panel'=16] {'panel'}, dimensions={1}, use_global_device_ids=true | all-gather | bytes 139264 | tf_op jit(solution)/shard_map/all_gather | solution.py:31
  1021.5 13.1 %collective-permute-start.11 = (bf16[32,2048]{1,0:T(8,128)(2,1)S(1)}, bf16[32,2048]{1,0:T(8,128)(2,1)S(1)}, u32[]{:S(2)}, u32[]{:S(2)}) collective-permute-start(bf16[32,2048]{1,0:T(8,128)(2,1)S(1)} %all_gather.34), channel_id=1, source_target_pairs={{0,16},{16,32},{32,48},{48,64},{64,80},{80,96},{96,112},{1,17},{17... | collective-permute-start | bytes 393224 | tf_op jit(solution)/shard_map/ppermute | solution.py:12
  1034.7 1.9 collective-permute-done.11
  1036.9 6.2 gather_fusion.3
  1043.8 17.5 %all_gather.35 = bf16[32,2048]{1,0:T(8,128)(2,1)S(1)} all-gather(bf16[32,128]{1,0:T(8,128)(2,1)S(1)} %fusion.6), channel_id=1, replica_groups=mesh['leaf'=8,'panel'=16] {'panel'}, dimensions={1}, use_global_device_ids=true | all-gather | bytes 139264 | tf_op jit(solution)/shard_map/all_gather | solution.py:149
  (120 shorter events, 21.8 us)
Async XLA Ops:
  7.2 77.7 %copy-start = (bf16[1,128,2048]{2,1,0:T(8,128)(2,1)S(1)}, bf16[1,128,2048]{2,1,0:T(8,128)(2,1)}, u32[]{:S(2)}) copy-start(bf16[1,128,2048]{2,1,0:T(8,128)(2,1)} %param.46) | copy-start | bytes 1572868
  7.2 77.7 %reduce-scatter.6.cloned.1.call-start = ((), (), s32[]{:S(2)}) async-start(), calls=%async_computation.5 | async-start | bytes 278528 | tf_op jit(solution)/shard_map/reduce_scatter | solution.py:76
  9.2 0.7 copy-start.10
  9.3 173.8 %all-reduce.5.cloned.1.call-start = ((), (), s32[]{:S(2)}) async-start(), calls=%async_computation.6 | async-start | bytes 524288 | tf_op jit(solution)/shard_map/psum | solution.py:21
  97.9 95.1 %copy-start.1 = (bf16[1,128,2048]{2,1,0:T(8,128)(2,1)S(1)}, bf16[1,128,2048]{2,1,0:T(8,128)(2,1)}, u32[]{:S(2)}) copy-start(bf16[1,128,2048]{2,1,0:T(8,128)(2,1)} %param.47) | copy-start | bytes 1572868
  98.9 163.9 %reduce-scatter.8.cloned.1.call-start = ((), (), s32[]{:S(2)}) async-start(), calls=%async_computation.7 | async-start | bytes 278528 | tf_op jit(solution)/shard_map/reduce_scatter | solution.py:94
  183.0 9.2 collective-permute-start
  186.9 5.3 copy-start.8
  193.0 70.6 %copy-start.2 = (bf16[1,128,2048]{2,1,0:T(8,128)(2,1)S(1)}, bf16[1,128,2048]{2,1,0:T(8,128)(2,1)}, u32[]{:S(2)}) copy-start(bf16[1,128,2048]{2,1,0:T(8,128)(2,1)} %param.48) | copy-start | bytes 1572868
  193.0 0.7 copy-start.4
  193.8 168.5 %all-reduce.7.cloned.1.call-start = ((), (), s32[]{:S(2)}) async-start(), calls=%async_computation.8 | async-start | bytes 524288 | tf_op jit(solution)/shard_map/psum | solution.py:21
  193.8 69.7 %copy-start.9 = (s32[1,2048]{1,0:T(1,128)S(1)}, s32[1,2048]{1,0:T(1,128)}, u32[]{:S(2)}) copy-start(s32[1,2048]{1,0:T(1,128)} %param.51) | copy-start | bytes 24580
  264.7 181.1 %reduce-scatter.10.cloned.1.call-start = ((), (), s32[]{:S(2)}) async-start(), calls=%async_computation.9 | async-start | bytes 278528 | tf_op jit(solution)/shard_map/reduce_scatter | solution.py:94
  362.2 8.6 collective-permute-start.1
  367.2 7.9 collective-permute-start.2
  376.1 0.7 copy-start.5
  376.1 69.7 %copy-start.11 = (f32[32,128]{1,0:T(8,128)S(1)}, f32[32,128]{1,0:T(8,128)}, u32[]{:S(2)}) copy-start(f32[32,128]{1,0:T(8,128)} %reduce-scatter.8.cloned.1.call-done) | copy-start | bytes 49156
  376.8 165.9 %all-reduce.9.cloned.1.call-start = ((), (), s32[]{:S(2)}) async-start(), calls=%async_computation.10 | async-start | bytes 524288 | tf_op jit(solution)/shard_map/psum | solution.py:21
  461.0 165.2 %reduce-scatter.12.cloned.1.call-start = ((), (), s32[]{:S(2)}) async-start(), calls=%async_computation.11 | async-start | bytes 278528 | tf_op jit(solution)/shard_map/reduce_scatter | solution.py:94
  542.7 7.0 collective-permute-start.3
  545.8 7.6 collective-permute-start.4
  553.5 0.7 copy-start.6
  554.3 167.3 %all-reduce.11.cloned.1.call-start = ((), (), s32[]{:S(2)}) async-start(), calls=%async_computation.12 | async-start | bytes 524288 | tf_op jit(solution)/shard_map/psum | solution.py:21
  628.0 175.5 %reduce-scatter.14.cloned.1.call-start = ((), (), s32[]{:S(2)}) async-start(), calls=%async_computation.13 | async-start | bytes 278528 | tf_op jit(solution)/shard_map/reduce_scatter | solution.py:94
  721.6 8.5 collective-permute-start.5
  730.1 0.7 copy-start.7
  730.1 73.4 %copy-start.14 = (f32[32,128]{1,0:T(8,128)S(1)}, f32[32,128]{1,0:T(8,128)}, u32[]{:S(2)}) copy-start(f32[32,128]{1,0:T(8,128)} %param.44) | copy-start | bytes 49156
  730.9 72.7 %copy-start.12 = (f32[32,128]{1,0:T(8,128)S(1)}, f32[32,128]{1,0:T(8,128)}, u32[]{:S(2)}) copy-start(f32[32,128]{1,0:T(8,128)} %reduce-scatter.12.cloned.1.call-done) | copy-start | bytes 49156
  837.7 7.2 collective-permute-start.6
  885.5 6.1 collective-permute-start.7
  886.8 6.3 collective-permute-start.8
  933.9 42.2 %collective-permute-start.10 = (bf16[32,2048]{1,0:T(8,128)(2,1)S(1)}, bf16[32,2048]{1,0:T(8,128)(2,1)S(1)}, u32[]{:S(2)}, u32[]{:S(2)}) collective-permute-start(bf16[32,2048]{1,0:T(8,128)(2,1)S(1)} %all_gather.32), channel_id=1, source_target_pairs={{0,16},{16,32},{32,48},{48,64},{64,80},{80,96},{96,112},{1,17},{17... | collective-permute-start | bytes 393224 | tf_op jit(solution)/shard_map/ppermute | solution.py:12
  974.2 6.3 collective-permute-start.9
  1021.5 15.1 %collective-permute-start.11 = (bf16[32,2048]{1,0:T(8,128)(2,1)S(1)}, bf16[32,2048]{1,0:T(8,128)(2,1)S(1)}, u32[]{:S(2)}, u32[]{:S(2)}) collective-permute-start(bf16[32,2048]{1,0:T(8,128)(2,1)S(1)} %all_gather.34), channel_id=1, source_target_pairs={{0,16},{16,32},{32,48},{48,64},{64,80},{80,96},{96,112},{1,17},{17... | collective-permute-start | bytes 393224 | tf_op jit(solution)/shard_map/ppermute | solution.py:12
  1036.9 6.2 copy-start.13
  1036.9 6.2 copy-start.15
  1043.1 18.1 %copy-start.3 = (bf16[1,128,2048]{2,1,0:T(8,128)(2,1)S(1)}, bf16[1,128,2048]{2,1,0:T(8,128)(2,1)}, u32[]{:S(2)}) copy-start(bf16[1,128,2048]{2,1,0:T(8,128)(2,1)} %param.45) | copy-start | bytes 1572868
Sparse Core Ops, SparseCore 0:
  11.2 73.6 reduce-scatter.5
  99.0 83.9 all-reduce.4
  193.9 68.8 reduce-scatter.7
  266.2 96.0 all-reduce.6
  376.9 68.8 reduce-scatter.9
  461.1 81.5 all-reduce.8
  554.4 71.7 reduce-scatter.11
  629.7 91.8 all-reduce.10
  731.0 72.4 reduce-scatter.13
where the time goes:
time: 1080 us; the launch traced here: 1070 us
  waiting for transfers between devices  749 us (69%)
  blocking collectives  151 us (14%)
  starting transfers between devices  82.5 us (8%)
  local copies, waits for them, and re-layouts  33.9 us (3%)
  other arithmetic  30 us (3%)
  between operations  15.2 us (1%)
    psum x4, waiting for transfers between devices, lifted(): summed = lax.psum(mapped, 'panel')  357 us
    reduce_scatter x4, waiting for transfers between devices, shards(): lax.psum_scatter(partial_value, 'panel', scatter_dimension=1, tiled=True)  282 us
    ppermute x12, starting transfers between devices, shifted(): lax.ppermute(value, axis, [(source, source + steps) for source in range(i...  82.2 us
    reduce_scatter x1, waiting for transfers between devices, shards(): lax.psum_scatter(leaf_partial, 'panel', scatter_dimension=1, tiled=True)  74.9 us
    all_gather x4, blocking collectives, shards(): whole_residual = lax.all_gather(residual, 'panel', axis=1, tiled=True)  68.1 us
    all_gather x4, blocking collectives, publish(): outgoing = lax.all_gather(sample_rows, 'panel', axis=1, tiled=True)  65.9 us
    ppermute x12, waiting for transfers between devices, shifted(): lax.ppermute(value, axis, [(source, source + steps) for source in range(i...  34.6 us
    scatter-add x2, other arithmetic, spread(): return blank_sum.at[:, targets].add(values)  23.8 us
  transfers between devices with their start and end apart: 21, of which 20 were waited for; matrix products, arithmetic and copies ran while one was open for 0% of the time, Pallas kernels for 0%

commit v1 on v0

v1 whole, which is shorter than its diff:
```python
import jax
import jax.numpy as jnp
from jax import lax
from jax.experimental import pallas as pl
from jax.experimental.pallas import tpu as pltpu
from jax.sharding import PartitionSpec as P

MESH = pl.DeviceIdType.MESH
BF16 = jnp.bfloat16
F32 = jnp.float32
PANELS = 16
SIDE = 4
ROWS = 128
WIDTH = 2048
SAMPLES = 32
MAP_TILE = 256
PARTS = PANELS * 2


def nn(left, right):
    return jnp.dot(left, right, preferred_element_type=F32)


def nt(left, right):
    return lax.dot_general(left, right, (((1,), (1,)), ((), ())), preferred_element_type=F32)


def kernel(
    leaf_source,
    leaf_noise,
    sep_source,
    sep_noise,
    leaf_inverse,
    leaf_coupling,
    sep_inverse,
    sep_coupling,
    sep_length,
    leaf_map,
    sep_map,
    leaf_sample,
    sep_sample,
    leaf_mapped,
    sep_mapped,
    leaf_rs_out,
    leaf_rs_in,
    leaf_up_out,
    leaf_up_in,
    sep_rs_out,
    sep_rs_in,
    sep_up_out,
    sep_up_in,
    residual_in,
    parent_in,
    sample_out,
    leaf_parent_in,
    leaf_residual_in,
    send_sems,
    recv_sems,
):
    m = lax.axis_index("leaf")
    p = lax.axis_index("panel")
    z = lax.div(p, SIDE)
    y = lax.rem(p, SIDE)
    even = lax.rem(m, 2) == 0
    second = lax.rem(m, 4) == 1
    third = m == 3
    top = m == 7
    inner = jnp.logical_or(second, third)
    rows = [lax.rem(z + step, SIDE) * SIDE for step in range(SIDE)]
    columns = [lax.rem(y + step, SIDE) for step in range(SIDE)]
    order = [(2, 2), (2, 1), (2, 3), (1, 2), (3, 2), (1, 1), (1, 3), (3, 1), (3, 3)]
    order += [(0, 2), (2, 0), (0, 1), (0, 3), (1, 0), (3, 0)]
    others = [rows[dz] + columns[dy] for dz, dy in order]
    everyone = others + [p]

    def copy(source, target, kind, leaf, panel):
        pltpu.make_async_remote_copy(
            src_ref=source,
            dst_ref=target,
            send_sem=send_sems.at[kind],
            recv_sem=recv_sems.at[kind],
            device_id=(leaf, panel),
            device_id_type=MESH,
        ).start()

    def await_parts(sem, count):
        span = leaf_up_in.at[pl.ds(0, count)]
        pltpu.make_async_copy(span, span, sem).wait()

    def scatter(value, out, into, base, kind, leaf, own):
        for q in range(PANELS):
            out[q] = value[:, q * ROWS : (q + 1) * ROWS].astype(BF16)
        for q in others:
            copy(out.at[q], into.at[base + p], kind, leaf, q)
        if own:
            into[base + p] = out[p]
        else:
            copy(out.at[p], into.at[base + p], kind, leaf, p)

    def total(into, first, count):
        summed = into[first].astype(F32)
        for index in range(first + 1, first + count):
            summed = summed + into[index].astype(F32)
        return summed

    def whole(into):
        return jnp.concatenate([into[index] for index in range(PANELS)], axis=1)

    def publish(share, into, kind):
        into[p] = share
        for q in others:
            copy(into.at[p], into.at[p], kind, m, q)

    def mapped(coupling, targets, out):
        def body(tile, carry):
            first = pl.multiple_of(tile * MAP_TILE, MAP_TILE)
            parent_row = lax.broadcasted_iota(jnp.int32, (MAP_TILE, WIDTH), 0) + first
            chosen = jnp.where(parent_row == targets[...], 1.0, 0.0).astype(BF16)
            out[:, pl.ds(first, MAP_TILE)] = nt(coupling[0], chosen).astype(BF16)
            return carry

        lax.fori_loop(0, WIDTH // MAP_TILE, body, 0)

    barrier = pltpu.get_barrier_semaphore()

    def greet(leaf):
        for q in everyone:
            pl.semaphore_signal(barrier, inc=1, device_id=(leaf, q), device_id_type=MESH)

    for q in others:
        pl.semaphore_signal(barrier, inc=1, device_id=(m, q), device_id_type=MESH)

    @pl.when(even)
    def _():
        greet(m + 1)

    @pl.when(jnp.logical_not(even))
    def _():
        greet(m - 1)

    @pl.when(lax.rem(m, 4) == 2)
    def _():
        greet(m - 1)

    @pl.when(second)
    def _():
        greet(m + 1)
        greet(3)

    @pl.when(third)
    def _():
        greet(1)
        greet(5)
        greet(7)

    @pl.when(top)
    def _():
        greet(3)

    leaf_partial = nn(leaf_source[...].astype(BF16), leaf_inverse[0])

    @pl.when(lax.rem(m, 4) == 0)
    def _():
        pl.semaphore_wait(barrier, 15 + 16)

    @pl.when(jnp.logical_or(lax.rem(m, 4) == 2, top))
    def _():
        pl.semaphore_wait(barrier, 15 + 32)

    @pl.when(second)
    def _():
        pl.semaphore_wait(barrier, 15 + 48)

    @pl.when(third)
    def _():
        pl.semaphore_wait(barrier, 15 + 64)

    scatter(leaf_partial, leaf_rs_out, leaf_rs_in, 0, 0, m, True)
    mapped(leaf_coupling, leaf_map, leaf_mapped)
    await_parts(recv_sems.at[0], 15)
    leaf_solved = total(leaf_rs_in, 0, PANELS)
    leaf_update = nn(leaf_solved.astype(BF16), leaf_mapped[...])

    @pl.when(even)
    def _():
        scatter(leaf_update, leaf_up_out, leaf_up_in, 0, 1, m, True)

    @pl.when(jnp.logical_not(even))
    def _():
        scatter(leaf_update, leaf_up_out, leaf_up_in, PANELS, 1, m - 1, False)

    mapped(sep_coupling, sep_map, sep_mapped)
    lane = lax.broadcasted_iota(jnp.int32, (1, ROWS), 1) + p * ROWS
    live = jnp.where(lane < sep_length[0], 1.0, 0.0)

    def front_forward(pending):
        right_side = (live * (sep_source[...] - pending)).astype(BF16)
        scatter(nn(right_side, sep_inverse[0]), sep_rs_out, sep_rs_in, 0, 2, m, True)

    @pl.when(even)
    def _():
        await_parts(recv_sems.at[1], 31)
        front_forward(total(leaf_up_in, 0, 32))

    @pl.when(inner)
    def _():
        await_parts(recv_sems.at[3], 32)
        front_forward(total(sep_up_in, 0, 32))

    @pl.when(top)
    def _():
        await_parts(recv_sems.at[3], 16)
        front_forward(total(sep_up_in, 0, 16))

    await_parts(recv_sems.at[2], 15)
    sep_solved = live * total(sep_rs_in, 0, PANELS)
    parent = jnp.where(third, 7, jnp.where(m == 1, 3, jnp.where(m == 5, 3, jnp.where(lax.rem(m, 4) == 0, m + 1, m - 1))))
    child = jnp.where(jnp.logical_or(m == 5, lax.rem(m, 4) == 2), PANELS, 0)

    @pl.when(jnp.logical_not(top))
    def _():
        update = nn(sep_solved.astype(BF16), sep_mapped[...])
        scatter(update, sep_up_out, sep_up_in, child, 3, parent, False)

    sep_wanted = sep_solved + sep_noise[...]

    @pl.when(jnp.logical_not(top))
    def _():
        await_parts(recv_sems.at[4], 16)
        correction = nt(whole(parent_in), sep_mapped[...])
        publish((live * (sep_wanted - correction)).astype(BF16), residual_in, 5)

    @pl.when(top)
    def _():
        publish((live * sep_wanted).astype(BF16), residual_in, 5)

    await_parts(recv_sems.at[5], 15)
    sample = live * nt(whole(residual_in), sep_inverse[0])
    sample_out[...] = sample.astype(BF16)

    def descend(leaf, into, kind):
        for q in everyone:
            copy(sample_out, into.at[p], kind, leaf, q)

    @pl.when(top)
    def _():
        descend(3, parent_in, 4)

    @pl.when(third)
    def _():
        descend(1, parent_in, 4)
        descend(5, parent_in, 4)

    @pl.when(second)
    def _():
        descend(m - 1, parent_in, 4)
        descend(m + 1, parent_in, 4)

    @pl.when(even)
    def _():
        leaf_parent_in[p] = sample_out[...]
        for q in others:
            copy(sample_out, leaf_parent_in.at[p], 6, m, q)
        descend(m + 1, leaf_parent_in, 6)

    sep_sample[...] = sample

    @pl.when(even)
    def _():
        await_parts(recv_sems.at[6], 15)

    @pl.when(jnp.logical_not(even))
    def _():
        await_parts(recv_sems.at[6], 16)

    leaf_correction = nt(whole(leaf_parent_in), leaf_mapped[...])
    leaf_residual = (leaf_solved + leaf_noise[...] - leaf_correction).astype(BF16)
    publish(leaf_residual, leaf_residual_in, 7)
    await_parts(recv_sems.at[7], 15)
    leaf_sample[...] = nt(whole(leaf_residual_in), leaf_inverse[0])

    for kind in (0, 2, 5, 7):
        await_parts(send_sems.at[kind], 15)

    @pl.when(even)
    def _():
        await_parts(send_sems.at[1], 15)
        await_parts(send_sems.at[6], 31)

    @pl.when(jnp.logical_not(even))
    def _():
        await_parts(send_sems.at[1], 16)

    @pl.when(jnp.logical_not(top))
    def _():
        await_parts(send_sems.at[3], 16)

    @pl.when(inner)
    def _():
        await_parts(send_sems.at[4], 32)

    @pl.when(top)
    def _():
        await_parts(send_sems.at[4], 16)


def shards(*arrays):
    vmem = pl.BlockSpec(memory_space=pltpu.VMEM)
    share = jax.ShapeDtypeStruct((SAMPLES, ROWS), F32)
    slots = pltpu.VMEM((PANELS, SAMPLES, ROWS), BF16)
    pair = pltpu.VMEM((2 * PANELS, SAMPLES, ROWS), BF16)
    slab = pltpu.VMEM((ROWS, WIDTH), BF16)
    one = pltpu.VMEM((SAMPLES, ROWS), BF16)
    return pl.pallas_call(
        kernel,
        out_shape=(share, share),
        in_specs=[vmem] * 8 + [pl.BlockSpec(memory_space=pltpu.SMEM)] + [vmem] * 2,
        out_specs=(vmem, vmem),
        scratch_shapes=[slab, slab]
        + [slots, slots, slots, pair]
        + [slots, slots, slots, pair]
        + [slots, slots, one, slots, slots]
        + [pltpu.SemaphoreType.DMA((8,)), pltpu.SemaphoreType.DMA((8,))],
        compiler_params=pltpu.CompilerParams(
            collective_id=0, has_side_effects=True, vmem_limit_bytes=32 * 1024 * 1024
        ),
    )(*arrays)


def solution(mesh):
    in_specs = (
        P(None, ("leaf", "panel")),
        P(None, ("leaf", "panel")),
        P(None, ("leaf", "panel")),
        P(None, ("leaf", "panel")),
        P("leaf", "panel", None),
        P("leaf", "panel", None),
        P("leaf", "panel", None),
        P("leaf", "panel", None),
        P("leaf"),
        P("leaf", None),
        P("leaf", None),
    )
    out_specs = (P(None, ("leaf", "panel")), P(None, ("leaf", "panel")))
    return jax.shard_map(shards, mesh=mesh, in_specs=in_specs, out_specs=out_specs, check_vma=False)
```

time: 1080 us -> 105 us (0.10); the launches traced: 1070 us -> 105 us
  waiting for transfers between devices: 749 us -> 0 us
  blocking collectives: 151 us -> 0 us
  Pallas kernels: 0 us -> 93.8 us
  starting transfers between devices: 82.5 us -> 0 us
  other arithmetic: 30 us -> 0 us
  local copies, waits for them, and re-layouts: 33.9 us -> 9.63 us
  between operations: 15.2 us -> 1.31 us
    reduce_scatter x5 -> x0, waiting for transfers between devices: 357 us -> none  [the longest x4 282 us: shards(): lax.psum_scatter(partial_value, 'panel', scatter_dimension=1, tiled=True)]
    psum x4 -> x0, waiting for transfers between devices: 357 us -> none  [lifted(): summed = lax.psum(mapped, 'panel')]
    all_gather x9 -> x0, blocking collectives: 151 us -> none  [the longest x4 68.1 us: shards(): whole_residual = lax.all_gather(residual, 'panel', axis=1, tiled=True)]
    pallas_call x0 -> x1, Pallas kernels: none -> 93.8 us  [shards(): pl.pallas_call(kernel, out_shape=(share, share), in_specs=[vmem] * 8 + [p...]
    ppermute x12 -> x0, starting transfers between devices: 82.2 us -> none  [shifted(): lax.ppermute(value, axis, [(source, source + steps) for source in range(i...]
    ppermute x12 -> x0, waiting for transfers between devices: 34.6 us -> none  [shifted(): lax.ppermute(value, axis, [(source, source + steps) for source in range(i...]
    gather x4 -> x0, local copies, waits for them, and re-layouts: 24.7 us -> none  [the longest x3 18.5 us: shards(): parent_view = jnp.take(arrived, sep_map[0], axis=1)]
    scatter-add x2 -> x0, other arithmetic: 23.8 us -> none  [spread(): return blank_sum.at[:, targets].add(values)]
  transfers between devices with their start and end apart: 21 -> 0, of which waited for: 20 -> 0; matrix products, arithmetic and copies ran while one was open for 0% -> 0% of each run, Pallas kernels for 0% -> 0%
where the time goes in v1:
time: 105 us
  Pallas kernels  93.8 us (89%)
  local copies, waits for them, and re-layouts  9.63 us (9%)
  between operations  1.31 us (1%)
    pallas_call x1, Pallas kernels, shards(): pl.pallas_call(kernel, out_shape=(share, share), in_specs=[vmem] * 8 + [p...  93.8 us
    unnamed x22, local copies, waits for them, and re-layouts  9.63 us

profile of v1, /device:TPU:1, one launch (start us, length us, event | category | flops | bytes accessed | tf_op | source)
XLA Modules:
  0.0 104.7 jit_solution(5788346556434399956)
XLA Ops:
  1.3 0.0 copy-start
  1.3 1.0 copy-done
  2.3 0.0 copy-start.1
  2.3 1.0 copy-done.1
  3.4 0.0 copy-start.2
  3.4 1.0 copy-done.2
  4.4 0.0 copy-start.3
  4.4 1.0 copy-done.3
  5.4 0.0 copy-start.4
  5.5 0.7 copy-done.4
  6.2 0.0 copy-start.5
  6.2 0.7 copy-done.5
  6.9 0.0 copy-start.6
  6.9 0.7 copy-done.6
  7.6 0.0 copy-start.7
  7.6 0.7 copy-done.7
  8.3 0.0 copy-start.8
  8.3 0.7 copy-done.8
  9.0 0.0 copy-start.9
  9.0 0.7 copy-done.9
  9.7 93.8 %shard_map.122 = (f32[32,128]{1,0:T(8,128)S(1)}, f32[32,128]{1,0:T(8,128)S(1)}) custom-call(f32[32,128]{1,0:T(8,128)S(1)} %copy-done.4, f32[32,128]{1,0:T(8,128)S(1)} %copy-done.5, f32[32,128]{1,0:T(8,128)S(1)} %copy-done.6, f32[32,128]{1,0:T(8,128)S(1)} %copy-done.7, bf16[1,128,2048]{2,1,0:T(8,128)(2,1)S(1)} %copy-done, ...), custom_call_target="tpu_custom_call" | custom-call | tf_op jit(solution)/shard_map/pallas_call | solution.py:314
  103.5 0.6 copy.16
  104.1 0.6 copy.17
Async XLA Ops:
  1.3 1.0 copy-start
  2.3 1.0 copy-start.1
  3.4 1.0 copy-start.2
  4.4 1.0 copy-start.3
  5.4 0.7 copy-start.4
  6.2 0.7 copy-start.5
  6.9 0.7 copy-start.6
  7.6 0.7 copy-start.7
  8.3 0.7 copy-start.8
  9.0 0.7 copy-start.9

commit v2 on v1

--- a/solution.py
+++ b/solution.py
@@ -26,6 +26,19 @@
 
 
 def kernel(
+    leaf_source_hbm,
+    leaf_noise_hbm,
+    sep_source_hbm,
+    sep_noise_hbm,
+    leaf_inverse_hbm,
+    leaf_coupling_hbm,
+    sep_inverse_hbm,
+    sep_coupling_hbm,
+    sep_length,
+    leaf_map_hbm,
+    sep_map_hbm,
+    leaf_sample,
+    sep_sample,
     leaf_source,
     leaf_noise,
     sep_source,
@@ -34,11 +47,9 @@
     leaf_coupling,
     sep_inverse,
     sep_coupling,
-    sep_length,
     leaf_map,
     sep_map,
-    leaf_sample,
-    sep_sample,
+    load_sems,
     leaf_mapped,
     sep_mapped,
     leaf_rs_out,
@@ -57,6 +68,25 @@
     send_sems,
     recv_sems,
 ):
+    loads = [
+        pltpu.make_async_copy(source, target, load_sems.at[index])
+        for index, (source, target) in enumerate(
+            (
+                (leaf_source_hbm, leaf_source),
+                (leaf_inverse_hbm, leaf_inverse),
+                (leaf_map_hbm, leaf_map),
+                (leaf_coupling_hbm, leaf_coupling),
+                (sep_map_hbm, sep_map),
+                (sep_coupling_hbm, sep_coupling),
+                (sep_source_hbm, sep_source),
+                (sep_inverse_hbm, sep_inverse),
+                (sep_noise_hbm, sep_noise),
+                (leaf_noise_hbm, leaf_noise),
+            )
+        )
+    ]
+    for load in loads:
+        load.start()
     m = lax.axis_index("leaf")
     p = lax.axis_index("panel")
     z = lax.div(p, SIDE)
@@ -157,6 +187,8 @@
     def _():
         greet(3)
 
+    for load in loads:
+        load.wait()
     leaf_partial = nn(leaf_source[...].astype(BF16), leaf_inverse[0])
 
     @pl.when(lax.rem(m, 4) == 0)
@@ -306,7 +338,11 @@
 
 def shards(*arrays):
     vmem = pl.BlockSpec(memory_space=pltpu.VMEM)
+    hbm = pl.BlockSpec(memory_space=pltpu.HBM)
     share = jax.ShapeDtypeStruct((SAMPLES, ROWS), F32)
+    vector = pltpu.VMEM((SAMPLES, ROWS), F32)
+    block = pltpu.VMEM((1, ROWS, WIDTH), BF16)
+    targets = pltpu.VMEM((1, WIDTH), jnp.int32)
     slots = pltpu.VMEM((PANELS, SAMPLES, ROWS), BF16)
     pair = pltpu.VMEM((2 * PANELS, SAMPLES, ROWS), BF16)
     slab = pltpu.VMEM((ROWS, WIDTH), BF16)
@@ -314,15 +350,19 @@
     return pl.pallas_call(
         kernel,
         out_shape=(share, share),
-        in_specs=[vmem] * 8 + [pl.BlockSpec(memory_space=pltpu.SMEM)] + [vmem] * 2,
+        in_specs=[hbm] * 8 + [pl.BlockSpec(memory_space=pltpu.SMEM)] + [hbm] * 2,
         out_specs=(vmem, vmem),
-        scratch_shapes=[slab, slab]
+        scratch_shapes=[vector] * 4
+        + [block] * 4
+        + [targets] * 2
+        + [pltpu.SemaphoreType.DMA((10,))]
+        + [slab, slab]
         + [slots, slots, slots, pair]
         + [slots, slots, slots, pair]
         + [slots, slots, one, slots, slots]
         + [pltpu.SemaphoreType.DMA((8,)), pltpu.SemaphoreType.DMA((8,))],
         compiler_params=pltpu.CompilerParams(
-            collective_id=0, has_side_effects=True, vmem_limit_bytes=32 * 1024 * 1024
+            collective_id=0, has_side_effects=True, vmem_limit_bytes=48 * 1024 * 1024
         ),
     )(*arrays)
 

time: 105 us -> 106 us (level)
  no operation moved by 1% of the time
where the time goes in v2:
time: 106 us; the launch traced here: 105 us
  Pallas kernels  94.2 us (89%)
  local copies, waits for them, and re-layouts  9.63 us (9%)
  between operations  1.31 us (1%)
    pallas_call x1, Pallas kernels, shards(): pl.pallas_call(kernel, out_shape=(share, share), in_specs=[hbm] * 8 + [pl...  94.2 us
    unnamed x22, local copies, waits for them, and re-layouts  9.63 us

profile of v2, /device:TPU:1, one launch (start us, length us, event | category | flops | bytes accessed | tf_op | source)
XLA Modules:
  0.0 105.1 jit_solution(16369031534621857561)
XLA Ops:
  1.3 0.0 copy-start
  1.3 1.0 copy-done
  2.3 0.0 copy-start.1
  2.3 1.0 copy-done.1
  3.4 0.0 copy-start.2
  3.4 1.0 copy-done.2
  4.4 0.0 copy-start.3
  4.4 1.0 copy-done.3
  5.4 0.0 copy-start.4
  5.5 0.7 copy-done.4
  6.2 0.0 copy-start.5
  6.2 0.7 copy-done.5
  6.9 0.0 copy-start.6
  6.9 0.7 copy-done.6
  7.6 0.0 copy-start.7
  7.6 0.7 copy-done.7
  8.3 0.0 copy-start.8
  8.3 0.7 copy-done.8
  9.0 0.0 copy-start.9
  9.0 0.7 copy-done.9
  9.7 94.2 %shard_map.122 = (f32[32,128]{1,0:T(8,128)S(1)}, f32[32,128]{1,0:T(8,128)S(1)}) custom-call(f32[32,128]{1,0:T(8,128)S(1)} %copy-done.4, f32[32,128]{1,0:T(8,128)S(1)} %copy-done.5, f32[32,128]{1,0:T(8,128)S(1)} %copy-done.6, f32[32,128]{1,0:T(8,128)S(1)} %copy-done.7, bf16[1,128,2048]{2,1,0:T(8,128)(2,1)S(1)} %copy-done, ...), custom_call_target="tpu_custom_call" | custom-call | tf_op jit(solution)/shard_map/pallas_call | solution.py:350
  103.9 0.6 copy.16
  104.5 0.6 copy.17
Async XLA Ops:
  1.3 1.0 copy-start
  2.3 1.0 copy-start.1
  3.4 1.0 copy-start.2
  4.4 1.0 copy-start.3
  5.4 0.7 copy-start.4
  6.2 0.7 copy-start.5
  6.9 0.7 copy-start.6
  7.6 0.7 copy-start.7
  8.3 0.7 copy-start.8
  9.0 0.7 copy-start.9

commit v3 on v2

--- a/solution.py
+++ b/solution.py
@@ -362,7 +362,7 @@
         + [slots, slots, one, slots, slots]
         + [pltpu.SemaphoreType.DMA((8,)), pltpu.SemaphoreType.DMA((8,))],
         compiler_params=pltpu.CompilerParams(
-            collective_id=0, has_side_effects=True, vmem_limit_bytes=48 * 1024 * 1024
+            collective_id=0, has_side_effects=True, vmem_limit_bytes=60 * 1024 * 1024
         ),
     )(*arrays)
 

time: 106 us -> 98.1 us (0.925)
  local copies, waits for them, and re-layouts: 9.63 us -> 1.94 us
    unnamed x22 -> x4, local copies, waits for them, and re-layouts: 9.63 us -> 1.94 us
where the time goes in v3:
time: 98.1 us; the launch traced here: 97.9 us
  Pallas kernels  94.6 us (96%)
  local copies, waits for them, and re-layouts  1.94 us (2%)
  between operations  1.3 us (1%)
    pallas_call x1, Pallas kernels, shards(): pl.pallas_call(kernel, out_shape=(share, share), in_specs=[hbm] * 8 + [pl...  94.6 us

profile of v3, /device:TPU:1, one launch (start us, length us, event | category | flops | bytes accessed | tf_op | source)
XLA Modules:
  0.0 97.9 jit_solution(5714973280257505652)
XLA Ops:
  1.3 94.6 %shard_map.122 = (f32[32,128]{1,0:T(8,128)}, f32[32,128]{1,0:T(8,128)}) custom-call(f32[32,128]{1,0:T(8,128)} %leaf_source_hbm.1, f32[32,128]{1,0:T(8,128)} %leaf_noise_hbm.1, f32[32,128]{1,0:T(8,128)} %sep_source_hbm.1, f32[32,128]{1,0:T(8,128)} %sep_noise_hbm.1, bf16[1,128,2048]{2,1,0:T(8,128)(2,1)} %leaf_inverse_hbm.1, ...), custom_call_target="tpu_custom_call" | custom-call | tf_op jit(solution)/shard_map/pallas_call | solution.py:350
  95.9 0.0 copy-start
  95.9 1.3 %copy.16 = f32[32,128]{1,0:T(8,128)} copy(f32[32,128]{1,0:T(8,128)} %get-tuple-element.4) | data formatting | bytes 32768
  97.2 0.0 copy-done
  97.2 0.6 copy.17
Async XLA Ops:
  95.9 1.3 %copy-start = (f32[32,128]{1,0:T(8,128)S(1)}, f32[32,128]{1,0:T(8,128)}, u32[]{:S(2)}) copy-start(f32[32,128]{1,0:T(8,128)} %get-tuple-element.5) | copy-start | bytes 49156

commit v4 on v3

v4 whole, which is shorter than its diff:
```python
import jax
import jax.numpy as jnp
from jax import lax
from jax.experimental import pallas as pl
from jax.experimental.pallas import tpu as pltpu
from jax.sharding import PartitionSpec as P

MESH = pl.DeviceIdType.MESH
BF16 = jnp.bfloat16
F32 = jnp.float32
PANELS = 16
SIDE = 4
ROWS = 128
GROUP = SIDE * ROWS
WIDTH = 2048
SAMPLES = 32
PART = 8
MAP_TILE = 256
LEAF_RS, LEAF_UP, SEP_RS, SEP_UP, DOWN, OUT, LEAF_DOWN, LEAF_RES = range(8)
NOISE, SOURCE, WANTED, M_NEAR, M_FAR, I_TURN, I_NEAR, I_FAR, L_NEAR, L_FAR = range(8, 18)
KINDS = 18


def nn(left, right):
    return jnp.dot(left, right, preferred_element_type=F32)


def nt(left, right):
    return lax.dot_general(left, right, (((1,), (1,)), ((), ())), preferred_element_type=F32)


def fold(value):
    half = value.shape[1] // 2
    return jnp.concatenate([value[:, :half], value[:, half:]], axis=0)


def unfold(value):
    return jnp.concatenate([value[:PART], value[PART:]], axis=1)


def total(into, first, count):
    summed = into[first].astype(F32)
    for index in range(first + 1, first + count):
        summed = summed + into[index].astype(F32)
    return summed


def kernel(
    leaf_source_hbm,
    leaf_noise_hbm,
    sep_source_hbm,
    sep_noise_hbm,
    leaf_inverse_hbm,
    leaf_coupling_hbm,
    sep_inverse_hbm,
    sep_coupling_hbm,
    sep_length,
    leaf_map_hbm,
    sep_map_hbm,
    leaf_sample,
    sep_sample,
    leaf_source,
    leaf_noise,
    sep_source,
    sep_noise,
    leaf_inverse,
    leaf_coupling,
    sep_inverse,
    sep_coupling,
    leaf_map,
    sep_map,
    load_sems,
    sep_rows,
    leaf_rows,
    turned,
    sep_columns,
    leaf_rs_out,
    leaf_rs_in,
    leaf_up_out,
    leaf_up_in,
    sep_rs_out,
    sep_rs_in,
    sep_up_out,
    sep_up_in,
    down_out,
    down_in,
    out_out,
    out_in,
    leaf_down_in,
    leaf_residual_in,
    source_in,
    noise_in,
    wanted_out,
    wanted_in,
    solved,
    send_sems,
    recv_sems,
):
    loads = [
        pltpu.make_async_copy(source, target, load_sems.at[index])
        for index, (source, target) in enumerate(
            (
                (leaf_source_hbm, leaf_source),
                (leaf_inverse_hbm, leaf_inverse),
                (sep_map_hbm, sep_map),
                (sep_coupling_hbm, sep_coupling),
                (sep_inverse_hbm, sep_inverse),
                (leaf_map_hbm, leaf_map),
                (leaf_coupling_hbm, leaf_coupling),
                (sep_source_hbm, sep_source),
                (sep_noise_hbm, sep_noise),
                (leaf_noise_hbm, leaf_noise),
            )
        )
    ]
    for load in loads:
        load.start()
    m = lax.axis_index("leaf")
    p = lax.axis_index("panel")
    z = lax.div(p, SIDE)
    y = lax.rem(p, SIDE)
    core = lax.rem(m, 2)
    even = core == 0
    odd = core == 1
    second = lax.rem(m, 4) == 1
    third = m == 3
    top = m == 7
    s = jnp.where(even, z, y)
    g = jnp.where(even, y, z)

    def place(parity, split, group):
        return split * (4 - 3 * parity) + group * (1 + 3 * parity)

    def step(value, by):
        return lax.rem(value + by, SIDE)

    zs = [step(z, by) * SIDE for by in range(SIDE)]
    ys = [step(y, by) for by in range(SIDE)]
    order = [(2, 2), (2, 1), (2, 3), (1, 2), (3, 2), (1, 1), (1, 3), (3, 1), (3, 3)]
    order += [(0, 2), (2, 0), (0, 1), (0, 3), (1, 0), (3, 0)]
    others = [zs[dz] + ys[dy] for dz, dy in order]

    def copy(source, target, kind, leaf, panel):
        pltpu.make_async_remote_copy(
            src_ref=source,
            dst_ref=target,
            send_sem=send_sems.at[kind],
            recv_sem=recv_sems.at[kind],
            device_id=(leaf, panel),
            device_id_type=MESH,
        ).start()

    spans = {4: source_in, 8: leaf_up_in, 32: sep_up_in, 128: sep_columns, 512: sep_rows}

    def settle(sem, size, count):
        span = spans[size].at[pl.ds(0, count)]
        pltpu.make_async_copy(span, span, sem).wait()

    def arrive(kind, size, count):
        settle(recv_sems.at[kind], size, count)

    def mapped(coupling, targets, out, slot):
        def body(tile, carry):
            first = pl.multiple_of(tile * MAP_TILE, MAP_TILE)
            parent_row = lax.broadcasted_iota(jnp.int32, (MAP_TILE, WIDTH), 0) + first
            chosen = jnp.where(parent_row == targets[...], 1.0, 0.0).astype(BF16)
            out[slot, :, pl.ds(first, MAP_TILE)] = nt(coupling[0], chosen).astype(BF16)
            return carry

        lax.fori_loop(0, WIDTH // MAP_TILE, body, 0)

    barrier = pltpu.get_barrier_semaphore()

    def greet(leaf, panel):
        pl.semaphore_signal(barrier, inc=1, device_id=(leaf, panel), device_id_type=MESH)

    def greet_front(leaf, parity):
        for group in range(SIDE):
            greet(leaf, place(parity, s, group))

    twin = m + 1 - 2 * core
    for q in others:
        greet(m, q)
    for q in others + [p]:
        greet(twin, q)

    @pl.when(lax.rem(m, 4) == 2)
    def _():
        greet_front(m - 1, 1)

    @pl.when(second)
    def _():
        greet_front(m + 1, 0)
        greet_front(3, 1)

    @pl.when(third)
    def _():
        greet_front(1, 1)
        greet_front(5, 1)
        greet_front(7, 1)

    @pl.when(top)
    def _():
        greet_front(3, 1)

    for load in loads[:2]:
        load.wait()
    leaf_partial = nn(leaf_source[...].astype(BF16), leaf_inverse[0])
    for q in range(PANELS):
        leaf_rs_out[q] = leaf_partial[:, q * ROWS : (q + 1) * ROWS].astype(BF16)
    leaf_rs_in[p] = leaf_rs_out[p]
    for load in loads[2:4]:
        load.wait()
    mapped(sep_coupling, sep_map, sep_rows, s)
    for load in loads[4:]:
        load.wait()

    @pl.when(even)
    def _():
        for group in range(SIDE):
            for k in range(SIDE):
                first = (k * SIDE + group) * ROWS
                turned[group, :, k * ROWS : (k + 1) * ROWS] = sep_inverse[0, :, first : first + ROWS]

    @pl.when(odd)
    def _():
        for group in range(SIDE):
            turned[group] = sep_inverse[0, :, group * GROUP : (group + 1) * GROUP]

    sep_columns[p] = turned[g]
    noise_in[s] = sep_noise[pl.ds(pl.multiple_of(s * PART, PART), PART), :]
    source_in[p] = sep_source[pl.ds(pl.multiple_of(s * PART, PART), PART), :]

    def rows_near(first, count):
        for by in (1, 3):
            copy(
                sep_rows.at[s, pl.ds(first, count)],
                sep_rows.at[s, pl.ds(first, count)],
                M_NEAR,
                m,
                place(core, step(s, by), g),
            )

    def rows_far():
        arrive(M_NEAR, 512, 2)
        for by, first in ((1, 0), (3, ROWS // 2)):
            slot = step(s, 4 - by)
            part = sep_rows.at[slot, pl.ds(first, ROWS // 2)]
            copy(part, part, M_FAR, m, place(core, step(s, by), g))

    def columns_turn():
        for by in (2, 1, 3):
            group = step(g, by)
            copy(turned.at[group], sep_columns.at[p], I_TURN, m, place(core, s, group))

    def columns_near():
        arrive(I_TURN, 128, 3)
        for group in range(SIDE):
            for by in (1, 3):
                part = sep_columns.at[place(core, s, group)]
                copy(part, part, I_NEAR, m, place(core, step(s, by), g))

    def columns_far():
        arrive(I_NEAR, 128, 8)
        for by, first in ((1, 0), (3, 2)):
            for group in (first, first + 1):
                part = sep_columns.at[place(core, step(s, 4 - by), group)]
                copy(part, part, I_FAR, m, place(core, step(s, by), g))

    def leaf_rows_near():
        for by in (1, 3):
            copy(leaf_rows.at[z], leaf_rows.at[z], L_NEAR, m, zs[by] + y)

    def leaf_rows_far():
        copy(leaf_rows.at[z], leaf_rows.at[z], L_FAR, m, zs[2] + y)

    @pl.when(lax.rem(m, 4) == 0)
    def _():
        pl.semaphore_wait(barrier, 31)

    @pl.when(jnp.logical_or(lax.rem(m, 4) == 2, top))
    def _():
        pl.semaphore_wait(barrier, 35)

    @pl.when(second)
    def _():
        pl.semaphore_wait(barrier, 39)

    @pl.when(third)
    def _():
        pl.semaphore_wait(barrier, 43)

    for q in others:
        copy(leaf_rs_out.at[q], leaf_rs_in.at[p], LEAF_RS, m, q)
    for by in (2, 1, 3):
        there = step(s, by)
        part = sep_noise.at[pl.ds(pl.multiple_of(there * PART, PART), PART)]
        copy(part, noise_in.at[s], NOISE, m, place(core, there, g))

    @pl.when(odd)
    def _():
        for dz, dy in order:
            part = sep_source.at[pl.ds(pl.multiple_of(ys[dy] * PART, PART), PART)]
            copy(part, source_in.at[p], SOURCE, m, zs[dz] + ys[dy])
        columns_turn()
        rows_near(0, ROWS)

    @pl.when(even)
    def _():
        rows_near(0, ROWS // 2)

    mapped(leaf_coupling, leaf_map, leaf_rows, z)
    arrive(LEAF_RS, 8, 15)
    leaf_solved = total(leaf_rs_in, 0, PANELS)
    leaf_update = nn(leaf_solved.astype(BF16), leaf_rows[z])
    for q in range(PANELS):
        leaf_up_out[q] = leaf_update[:, q * ROWS : (q + 1) * ROWS].astype(BF16)

    @pl.when(even)
    def _():
        for q in others:
            copy(leaf_up_out.at[q], leaf_up_in.at[p], LEAF_UP, m, q)
        leaf_up_in[p] = leaf_up_out[p]
        rows_near(ROWS // 2, ROWS // 2)

    @pl.when(odd)
    def _():
        for q in others + [p]:
            copy(leaf_up_out.at[q], leaf_up_in.at[PANELS + p], LEAF_UP, m - 1, q)

    wanted_out[...] = leaf_solved + leaf_noise[...]
    wanted_in[z] = wanted_out[pl.ds(pl.multiple_of(z * PART, PART), PART), :]
    for by in (2, 1, 3):
        part = wanted_out.at[pl.ds(pl.multiple_of(step(z, by) * PART, PART), PART)]
        copy(part, wanted_in.at[z], WANTED, m, zs[by] + y)

    length = sep_length[0]
    lane = lax.broadcasted_iota(jnp.int32, (1, ROWS), 1)
    live_own = jnp.where(lane + p * ROWS < length, 1.0, 0.0)
    live_group = jnp.concatenate(
        [jnp.where(lane + place(core, k, g) * ROWS < length, 1.0, 0.0) for k in range(SIDE)], axis=1
    )
    live_all = jnp.where(lax.broadcasted_iota(jnp.int32, (1, WIDTH), 1) < length, 1.0, 0.0)

    @pl.when(even)
    def _():
        arrive(LEAF_UP, 8, 31)
        pending = total(leaf_up_in, 0, 2 * PANELS)
        right_side = (live_own * (sep_source[...] - pending)).astype(BF16)
        partial = nn(right_side, sep_inverse[0])
        for split in range(SIDE):
            rows = partial[split * PART : (split + 1) * PART]
            for group in range(SIDE):
                firsts = [(k * SIDE + group) * ROWS for k in range(SIDE)]
                chunk = jnp.concatenate([rows[:, first : first + ROWS] for first in firsts], axis=1)
                sep_rs_out[split * SIDE + group] = fold(chunk).astype(BF16)
        for q in others:
            copy(sep_rs_out.at[q], sep_rs_in.at[p], SEP_RS, m, q)
        sep_rs_in[p] = sep_rs_out[p]
        rows_far()
        arrive(SEP_RS, 8, 15)
        solved[...] = live_group * unfold(total(sep_rs_in, 0, PANELS))

    def front_forward(count):
        pending = unfold(total(sep_up_in, 0, count))
        source = jnp.concatenate([source_in[q] for q in range(PANELS)], axis=1)
        right_side = (live_all * (source - pending)).astype(BF16)
        solved[...] = live_group * nn(right_side, sep_columns[...].reshape(WIDTH, GROUP))

    @pl.when(odd)
    def _():
        columns_near()
        rows_far()
        columns_far()
        leaf_rows_near()
        arrive(SOURCE, 4, 15)
        arrive(I_FAR, 128, 4)

    @pl.when(jnp.logical_or(second, third))
    def _():
        arrive(SEP_UP, 32, 8)
        front_forward(8)

    @pl.when(top)
    def _():
        arrive(SEP_UP, 32, 4)
        front_forward(4)

    arrive(M_FAR, 512, 1)
    first_child = jnp.logical_or(lax.rem(m, 4) == 0, jnp.logical_or(m == 1, third))
    slot = jnp.where(first_child, 0, SIDE) + g
    low_parent = jnp.where(lax.rem(m, 4) == 0, m + 1, m - 1)
    parent = jnp.where(third, 7, jnp.where(even, low_parent, 3))

    @pl.when(jnp.logical_not(top))
    def _():
        update = nn(solved[...].astype(BF16), sep_rows[...].reshape(GROUP, WIDTH))
        sep_up_out[...] = fold(update).astype(BF16)
        for group in range(SIDE):
            copy(sep_up_out, sep_up_in.at[slot], SEP_UP, parent, place(1, s, group))

    @pl.when(even)
    def _():
        columns_turn()
        columns_near()
        leaf_rows_near()
        leaf_rows_far()
        columns_far()
        arrive(I_FAR, 128, 4)

    @pl.when(jnp.logical_and(odd, jnp.logical_not(top)))
    def _():
        leaf_rows_far()

    arrive(NOISE, 4, 3)
    noise = jnp.concatenate([noise_in[k] for k in range(SIDE)], axis=1)

    @pl.when(jnp.logical_not(top))
    def _():
        arrive(DOWN, 32, 4)
        view = unfold(total(down_in, 0, SIDE)).astype(BF16)
        solved[...] = solved[...] - nt(view, sep_rows[...].reshape(GROUP, WIDTH))

    residual = (live_group * (solved[...] + noise)).astype(BF16)
    partial_sample = live_all * nt(residual, sep_columns[...].reshape(WIDTH, GROUP))
    down_out[...] = fold(partial_sample).astype(BF16)

    def descend(leaf, parity):
        for group in range(SIDE):
            copy(down_out, down_in.at[g], DOWN, leaf, place(parity, s, group))

    @pl.when(top)
    def _():
        descend(3, 1)
        leaf_rows_far()

    @pl.when(third)
    def _():
        descend(1, 1)
        descend(5, 1)

    @pl.when(second)
    def _():
        descend(m - 1, 0)
        descend(m + 1, 0)

    @pl.when(even)
    def _():
        for by in (2, 1, 3):
            copy(down_out, leaf_down_in.at[y], LEAF_DOWN, m, zs[0] + ys[by])
        for by in (2, 1, 3, 0):
            copy(down_out, leaf_down_in.at[y], LEAF_DOWN, m + 1, zs[0] + ys[by])
        leaf_down_in[y] = down_out[...]

    for q in range(PANELS):
        out_out[q] = partial_sample[:, q * ROWS : (q + 1) * ROWS]
    for q in others:
        copy(out_out.at[q], out_in.at[p], OUT, m, q)
    out_in[p] = out_out[p]
    arrive(L_NEAR, 512, 2)
    arrive(L_FAR, 512, 1)
    arrive(WANTED, 4, 3)

    @pl.when(even)
    def _():
        arrive(LEAF_DOWN, 32, 3)

    @pl.when(odd)
    def _():
        arrive(LEAF_DOWN, 32, 4)

    leaf_view = unfold(total(leaf_down_in, 0, SIDE)).astype(BF16)
    correction = nt(leaf_view, leaf_rows[...].reshape(GROUP, WIDTH))
    wanted = jnp.concatenate([wanted_in[k] for k in range(SIDE)], axis=1)
    leaf_residual_in[p] = fold(wanted - correction).astype(BF16)
    for q in others:
        copy(leaf_residual_in.at[p], leaf_residual_in.at[p], LEAF_RES, m, q)
    arrive(OUT, 4, 15)
    for split in range(SIDE):
        if_even = total(out_in, split * SIDE, SIDE)
        if_odd = out_in[split] + out_in[split + 4] + out_in[split + 8] + out_in[split + 12]
        sep_sample[split * PART : (split + 1) * PART, :] = jnp.where(even, if_even, if_odd)
    arrive(LEAF_RES, 8, 15)
    pieces = [unfold(leaf_residual_in[q].astype(F32)) for q in range(PANELS)]
    blocks = []
    for q in range(PANELS):
        k, group = q // SIDE, q % SIDE
        cut = [pieces[split * SIDE + group][:, k * ROWS : (k + 1) * ROWS] for split in range(SIDE)]
        blocks.append(jnp.concatenate(cut, axis=0).astype(BF16))
    leaf_sample[...] = nt(jnp.concatenate(blocks, axis=1), leaf_inverse[0])

    def sent(kind, size, count):
        settle(send_sems.at[kind], size, count)

    sent(LEAF_RS, 8, 15)
    sent(OUT, 4, 15)
    sent(LEAF_RES, 8, 15)
    sent(NOISE, 4, 3)
    sent(WANTED, 4, 3)
    sent(M_NEAR, 512, 2)
    sent(M_FAR, 512, 1)
    sent(I_TURN, 128, 3)
    sent(I_NEAR, 128, 8)
    sent(I_FAR, 128, 4)
    sent(L_NEAR, 512, 2)
    sent(L_FAR, 512, 1)

    @pl.when(even)
    def _():
        sent(LEAF_UP, 8, 15)
        sent(SEP_RS, 8, 15)
        sent(LEAF_DOWN, 32, 7)

    @pl.when(odd)
    def _():
        sent(LEAF_UP, 8, 16)
        sent(SOURCE, 4, 15)

    @pl.when(jnp.logical_not(top))
    def _():
        sent(SEP_UP, 32, 4)

    @pl.when(jnp.logical_or(second, third))
    def _():
        sent(DOWN, 32, 8)

    @pl.when(top)
    def _():
        sent(DOWN, 32, 4)


def shards(*arrays):
    vmem = pl.BlockSpec(memory_space=pltpu.VMEM)
    hbm = pl.BlockSpec(memory_space=pl.ANY)
    share = jax.ShapeDtypeStruct((SAMPLES, ROWS), F32)
    vector = pltpu.VMEM((SAMPLES, ROWS), F32)
    block = pltpu.VMEM((1, ROWS, WIDTH), BF16)
    targets = pltpu.VMEM((1, WIDTH), jnp.int32)
    slots = pltpu.VMEM((PANELS, SAMPLES, ROWS), BF16)
    split = pltpu.VMEM((PANELS, 2 * PART, GROUP // 2), BF16)
    rows = pltpu.VMEM((SIDE, ROWS, WIDTH), BF16)
    partial = (2 * PART, WIDTH // 2)
    pieces = pltpu.VMEM((PANELS, PART, ROWS), F32)
    ring = pltpu.VMEM((SIDE, PART, ROWS), F32)
    return pl.pallas_call(
        kernel,
        out_shape=(share, share),
        in_specs=[hbm] * 8 + [pl.BlockSpec(memory_space=pltpu.SMEM)] + [hbm] * 2,
        out_specs=(vmem, vmem),
        scratch_shapes=[vector] * 4
        + [block] * 4
        + [targets] * 2
        + [pltpu.SemaphoreType.DMA((10,))]
        + [rows, rows]
        + [pltpu.VMEM((SIDE, ROWS, GROUP), BF16), pltpu.VMEM((PANELS, ROWS, GROUP), BF16)]
        + [slots, slots, slots, pltpu.VMEM((2 * PANELS, SAMPLES, ROWS), BF16)]
        + [split, split]
        + [pltpu.VMEM(partial, BF16), pltpu.VMEM((2 * SIDE,) + partial, BF16)]
        + [pltpu.VMEM(partial, BF16), pltpu.VMEM((SIDE,) + partial, BF16)]
        + [pieces, pieces]
        + [pltpu.VMEM((SIDE,) + partial, BF16), split]
        + [pieces, ring, vector, ring, pltpu.VMEM((PART, GROUP), F32)]
        + [pltpu.SemaphoreType.DMA((KINDS,)), pltpu.SemaphoreType.DMA((KINDS,))],
        compiler_params=pltpu.CompilerParams(
            collective_id=0, has_side_effects=True, vmem_limit_bytes=60 * 1024 * 1024
        ),
    )(*arrays)


def solution(mesh):
    in_specs = (
        P(None, ("leaf", "panel")),
        P(None, ("leaf", "panel")),
        P(None, ("leaf", "panel")),
        P(None, ("leaf", "panel")),
        P("leaf", "panel", None),
        P("leaf", "panel", None),
        P("leaf", "panel", None),
        P("leaf", "panel", None),
        P("leaf"),
        P("leaf", None),
        P("leaf", None),
    )
    out_specs = (P(None, ("leaf", "panel")), P(None, ("leaf", "panel")))
    return jax.shard_map(shards, mesh=mesh, in_specs=in_specs, out_specs=out_specs, check_vma=False)
```

time: 98.1 us -> 86.4 us (0.88)
  Pallas kernels: 94.6 us -> 83 us
    pallas_call x1, Pallas kernels: 94.6 us -> 83 us  [shards(): pl.pallas_call(kernel, out_shape=(share, share), in_specs=[hbm] * 8 + [pl...]
where the time goes in v4:
time: 86.4 us; the launch traced here: 86.2 us
  Pallas kernels  83 us (96%)
  local copies, waits for them, and re-layouts  1.94 us (2%)
  between operations  1.3 us (2%)
    pallas_call x1, Pallas kernels, shards(): pl.pallas_call(kernel, out_shape=(share, share), in_specs=[hbm] * 8 + [pl...  83 us
    unnamed x4, local copies, waits for them, and re-layouts  1.94 us

profile of v4, /device:TPU:1, one launch (start us, length us, event | category | flops | bytes accessed | tf_op | source)
XLA Modules:
  0.0 86.2 jit_solution(1708285417035553604)
XLA Ops:
  1.3 83.0 %shard_map.122 = (f32[32,128]{1,0:T(8,128)}, f32[32,128]{1,0:T(8,128)}) custom-call(f32[32,128]{1,0:T(8,128)} %leaf_source_hbm.1, f32[32,128]{1,0:T(8,128)} %leaf_noise_hbm.1, f32[32,128]{1,0:T(8,128)} %sep_source_hbm.1, f32[32,128]{1,0:T(8,128)} %sep_noise_hbm.1, bf16[1,128,2048]{2,1,0:T(8,128)(2,1)} %leaf_inverse_hbm.1, ...), custom_call_target="tpu_custom_call" | custom-call | tf_op jit(solution)/shard_map/pallas_call | solution.py:545
  84.3 0.0 copy-start
  84.3 1.3 %copy.16 = f32[32,128]{1,0:T(8,128)} copy(f32[32,128]{1,0:T(8,128)} %get-tuple-element.4) | data formatting | bytes 32768
  85.6 0.0 copy-done
  85.6 0.6 copy.17
Async XLA Ops:
  84.3 1.3 %copy-start = (f32[32,128]{1,0:T(8,128)S(1)}, f32[32,128]{1,0:T(8,128)}, u32[]{:S(2)}) copy-start(f32[32,128]{1,0:T(8,128)} %get-tuple-element.5) | copy-start | bytes 49156

commit v5 on v4

v5 whole, which is shorter than its diff:
```python
import jax
import jax.numpy as jnp
from jax import lax
from jax.experimental import pallas as pl
from jax.experimental.pallas import tpu as pltpu
from jax.sharding import PartitionSpec as P

MESH = pl.DeviceIdType.MESH
BF16 = jnp.bfloat16
F32 = jnp.float32
PANELS = 16
SIDE = 4
ROWS = 128
GROUP = SIDE * ROWS
WIDTH = 2048
SAMPLES = 32
PART = 8
MAP_TILE = 256
HALVES = 4
HALF = WIDTH // HALVES
LEAF_RS, LEAF_UP, SEP_RS, LOW_UP, OUT, LEAF_RES, NOISE, SOURCE, WANTED, SEP_RES, SAMPLE = range(11)
M_NEAR, M_FAR, I_TURN, I_NEAR, I_FAR = range(11, 16)
SEP_UP, DOWN = range(16, 24, HALVES)
KINDS = 24


def nn(left, right):
    return jnp.dot(left, right, preferred_element_type=F32)


def nt(left, right):
    return lax.dot_general(left, right, (((1,), (1,)), ((), ())), preferred_element_type=F32)


def fold(value):
    half = value.shape[1] // 2
    return jnp.concatenate([value[:, :half], value[:, half:]], axis=0)


def unfold(value):
    return jnp.concatenate([value[:PART], value[PART:]], axis=1)


def slab(rows, k, first=0, count=ROWS):
    return rows.at[pl.ds(pl.multiple_of(k * ROWS + first, ROWS // 2), count)]


def total(into, first, count):
    summed = into[first].astype(F32)
    for index in range(first + 1, first + count):
        summed = summed + into[index].astype(F32)
    return summed


def kernel(
    leaf_source_hbm,
    leaf_noise_hbm,
    sep_source_hbm,
    sep_noise_hbm,
    leaf_inverse_hbm,
    leaf_coupling_hbm,
    sep_inverse_hbm,
    sep_coupling_hbm,
    sep_length,
    leaf_map_hbm,
    sep_map_hbm,
    leaf_sample,
    sep_sample,
    leaf_source,
    leaf_noise,
    sep_source,
    sep_noise,
    leaf_inverse,
    leaf_coupling,
    sep_inverse,
    sep_coupling,
    leaf_map,
    sep_map,
    load_sems,
    sep_rows,
    leaf_rows,
    turned,
    sep_columns,
    leaf_rs_out,
    leaf_rs_in,
    leaf_up_out,
    leaf_up_in,
    sep_rs_out,
    sep_rs_in,
    low_up_out,
    low_up_in,
    parts_out,
    parts_in,
    sep_up_out,
    sep_up_in,
    down_out,
    down_in,
    out_out,
    out_in,
    sample_in,
    leaf_residual_in,
    source_in,
    wanted_out,
    wanted_in,
    solved,
    send_sems,
    recv_sems,
):
    loads = [
        pltpu.make_async_copy(source, target, load_sems.at[index])
        for index, (source, target) in enumerate(
            (
                (leaf_source_hbm, leaf_source),
                (leaf_inverse_hbm, leaf_inverse),
                (leaf_map_hbm, leaf_map),
                (leaf_coupling_hbm, leaf_coupling),
                (sep_map_hbm, sep_map),
                (sep_coupling_hbm, sep_coupling),
                (sep_inverse_hbm, sep_inverse),
                (sep_source_hbm, sep_source),
                (sep_noise_hbm, sep_noise),
                (leaf_noise_hbm, leaf_noise),
            )
        )
    ]
    for load in loads:
        load.start()
    m = lax.axis_index("leaf")
    p = lax.axis_index("panel")
    z = lax.div(p, SIDE)
    y = lax.rem(p, SIDE)
    core = lax.rem(m, 2)
    even = core == 0
    odd = core == 1
    second = lax.rem(m, 4) == 1
    third = m == 3
    top = m == 7
    inner = jnp.logical_or(second, third)

    def step(value, by):
        return lax.rem(value + by, SIDE)

    zs = [step(z, by) * SIDE for by in range(SIDE)]
    ys = [step(y, by) for by in range(SIDE)]
    order = [(2, 2), (2, 1), (2, 3), (1, 2), (3, 2), (1, 1), (1, 3), (3, 1), (3, 3)]
    order += [(0, 2), (2, 0), (0, 1), (0, 3), (1, 0), (3, 0)]
    others = [zs[dz] + ys[dy] for dz, dy in order]
    row = [zs[0] + ys[by] for by in (2, 1, 3, 0)]

    def copy(source, target, kind, leaf, panel):
        pltpu.make_async_remote_copy(
            src_ref=source,
            dst_ref=target,
            send_sem=send_sems.at[kind],
            recv_sem=recv_sems.at[kind],
            device_id=(leaf, panel),
            device_id_type=MESH,
        ).start()

    spans = {4: source_in, 8: leaf_up_in, 16: sep_up_in.at[0], 128: sep_columns}

    def settle(sem, size, count):
        span = spans[size].at[pl.ds(0, count)]
        pltpu.make_async_copy(span, span, sem).wait()

    def arrive(kind, size, count):
        settle(recv_sems.at[kind], size, count)

    def sent(kind, size, count):
        settle(send_sems.at[kind], size, count)

    def mapped(coupling, targets, out):
        row = lax.broadcasted_iota(jnp.int32, (MAP_TILE, ROWS), 0).astype(jnp.int16)
        row = jnp.concatenate([row] * (WIDTH // ROWS), axis=1)
        one = jnp.ones((MAP_TILE, WIDTH), BF16)

        def body(tile, carry):
            first = pl.multiple_of(tile * MAP_TILE, MAP_TILE)
            target = jnp.broadcast_to(targets[...] - first, (MAP_TILE, WIDTH)).astype(jnp.int16)
            chosen = jnp.where(row == target, one, jnp.zeros_like(one))
            out[:, pl.ds(first, MAP_TILE)] = nt(chosen, coupling[0]).T.astype(BF16)
            return carry

        lax.fori_loop(0, WIDTH // MAP_TILE, body, 0)

    barrier = pltpu.get_barrier_semaphore()

    def greet(leaf, panel):
        pl.semaphore_signal(barrier, inc=1, device_id=(leaf, panel), device_id_type=MESH)

    def greet_front(leaf):
        for q in row:
            greet(leaf, q)

    @pl.when(lax.rem(m, 4) == 2)
    def _():
        for q in others + [p]:
            greet(m - 1, q)

    @pl.when(second)
    def _():
        for q in others + [p]:
            greet(m + 1, q)
        greet_front(3)

    @pl.when(third)
    def _():
        greet_front(1)
        greet_front(5)
        greet_front(7)

    @pl.when(top)
    def _():
        greet_front(3)

    twin = m + 1 - 2 * core
    for q in others:
        greet(m, q)
        greet(twin, q)
    greet(twin, p)

    for load in loads[:2]:
        load.wait()
    leaf_partial = nn(leaf_source[...].astype(BF16), leaf_inverse[0])
    for q in range(PANELS):
        leaf_rs_out[q] = leaf_partial[:, q * ROWS : (q + 1) * ROWS].astype(BF16)
    leaf_rs_in[p] = leaf_rs_out[p]
    def prepare():
        for load in loads[4:8]:
            load.wait()
        mapped(sep_coupling, sep_map, slab(sep_rows, z))
        length = sep_length[0]
        row_live = lax.broadcasted_iota(jnp.int32, (ROWS, WIDTH), 0) + p * ROWS < length
        column_live = lax.broadcasted_iota(jnp.int32, (ROWS, WIDTH), 1) < length
        live = jnp.where(jnp.logical_and(row_live, column_live), 1.0, 0.0)
        sep_inverse[0] = sep_inverse[0] * live.astype(BF16)

    def mine(value_ref):
        return value_ref[pl.ds(pl.multiple_of(z * PART, PART), PART), :]

    @pl.when(odd)
    def _():
        prepare()
        for group in range(SIDE):
            for k in range(SIDE):
                first = (k * SIDE + group) * ROWS
                turned[group, :, k * ROWS : (k + 1) * ROWS] = sep_inverse[0, :, first : first + ROWS]
        sep_columns[p] = turned[y]
        source_in[p] = mine(sep_source)

    for load in loads[2:4] + loads[8:]:
        load.wait()

    def rows_near():
        part = slab(sep_rows, z)
        for by in (1, 3):
            copy(part, part, M_NEAR, m, zs[by] + y)

    def rows_far():
        arrive(M_NEAR, 128, 8)
        for by, first in ((1, 0), (3, ROWS // 2)):
            part = slab(sep_rows, step(z, 4 - by), first, ROWS // 2)
            copy(part, part, M_FAR, m, zs[by] + y)

    def columns_turn():
        for by in (2, 1, 3):
            copy(turned.at[ys[by]], sep_columns.at[p], I_TURN, m, zs[0] + ys[by])

    def columns_near():
        arrive(I_TURN, 128, 3)
        part = sep_columns.at[pl.ds(zs[0], SIDE)]
        for by in (1, 3):
            copy(part, part, I_NEAR, m, zs[by] + y)

    def columns_far():
        arrive(I_NEAR, 128, 8)
        for by, first in ((1, 0), (3, 2)):
            part = sep_columns.at[pl.ds(zs[4 - by] + first, 2)]
            copy(part, part, I_FAR, m, zs[by] + y)

    def spread(out, into, base, kind, leaf, own):
        for q in others:
            copy(out.at[q], into.at[base + p], kind, leaf, q)
        if own:
            into[base + p] = out[p]
        else:
            copy(out.at[p], into.at[base + p], kind, leaf, p)

    def cut_columns(value, out):
        for q in range(PANELS):
            out[q] = value[:, q * ROWS : (q + 1) * ROWS].astype(BF16)

    def cut_parts(value, out):
        for split in range(SIDE):
            rows = value[split * PART : (split + 1) * PART]
            for group in range(SIDE):
                firsts = [(k * SIDE + group) * ROWS for k in range(SIDE)]
                chunk = jnp.concatenate([rows[:, first : first + ROWS] for first in firsts], axis=1)
                out[split * SIDE + group] = fold(chunk).astype(BF16)

    def joined_columns(into):
        return jnp.concatenate([into[q] for q in range(PANELS)], axis=1)

    def joined_parts(into):
        pieces = [unfold(into[q].astype(F32)) for q in range(PANELS)]
        blocks = []
        for q in range(PANELS):
            k, group = q // SIDE, q % SIDE
            cut = [pieces[split * SIDE + group][:, k * ROWS : (k + 1) * ROWS] for split in range(SIDE)]
            blocks.append(jnp.concatenate(cut, axis=0).astype(BF16))
        return jnp.concatenate(blocks, axis=1)

    @pl.when(lax.rem(m, 4) == 0)
    def _():
        pl.semaphore_wait(barrier, 31)

    @pl.when(lax.rem(m, 4) == 2)
    def _():
        pl.semaphore_wait(barrier, 47)

    @pl.when(top)
    def _():
        pl.semaphore_wait(barrier, 35)

    @pl.when(second)
    def _():
        pl.semaphore_wait(barrier, 51)

    @pl.when(third)
    def _():
        pl.semaphore_wait(barrier, 43)

    for q in others:
        copy(leaf_rs_out.at[q], leaf_rs_in.at[p], LEAF_RS, m, q)

    @pl.when(odd)
    def _():
        columns_turn()
        rows_near()
        for by in (2, 1, 3):
            part = sep_noise.at[pl.ds(pl.multiple_of(step(z, by) * PART, PART), PART)]
            copy(part, wanted_in.at[z], NOISE, m, zs[by] + y)
        wanted_in[z] = mine(sep_noise)

    @pl.when(jnp.logical_or(third, top))
    def _():
        for dz, dy in order:
            part = sep_source.at[pl.ds(pl.multiple_of(step(z, dz) * PART, PART), PART)]
            copy(part, source_in.at[p], SOURCE, m, zs[dz] + ys[dy])

    mapped(leaf_coupling, leaf_map, leaf_rows)
    arrive(LEAF_RS, 8, 15)
    leaf_solved = total(leaf_rs_in, 0, PANELS)
    cut_columns(nn(leaf_solved.astype(BF16), leaf_rows[...]), leaf_up_out)

    @pl.when(even)
    def _():
        spread(leaf_up_out, leaf_up_in, 0, LEAF_UP, m, True)

    @pl.when(odd)
    def _():
        spread(leaf_up_out, leaf_up_in, PANELS, LEAF_UP, m - 1, False)

    low_parent = jnp.where(lax.rem(m, 4) == 0, m + 1, m - 1)
    low_slot = jnp.where(lax.rem(m, 4) == 0, 0, PANELS)

    @pl.when(even)
    def _():
        prepare()
        arrive(LEAF_UP, 8, 31)
        pending = total(leaf_up_in, 0, 2 * PANELS)
        cut_columns(nn((sep_source[...] - pending).astype(BF16), sep_inverse[0]), sep_rs_out)
        spread(sep_rs_out, sep_rs_in, 0, SEP_RS, m, True)
        arrive(SEP_RS, 8, 15)
        low_solved = total(sep_rs_in, 0, PANELS)
        cut_columns(nn(low_solved.astype(BF16), slab(sep_rows, z)[...]), low_up_out)
        spread(low_up_out, low_up_in, low_slot, LOW_UP, low_parent, False)
        wanted_out[...] = low_solved + sep_noise[...]
        wanted_in[z] = mine(wanted_out)
        for by in (2, 1, 3):
            part = wanted_out.at[pl.ds(pl.multiple_of(step(z, by) * PART, PART), PART)]
            copy(part, wanted_in.at[z], WANTED, m, zs[by] + y)
        rows_near()
        rows_far()
        arrive(M_FAR, 128, 4)
        arrive(WANTED, 4, 3)

    def columns_half(half):
        return sep_columns[half * PANELS // HALVES : (half + 1) * PANELS // HALVES].reshape(HALF, GROUP)

    def front_forward(count):
        found = jnp.zeros((PART, GROUP), F32)
        for half in range(HALVES):
            arrive(SEP_UP + half, 16, count)
            pending = unfold(total(sep_up_in.at[half], 0, count))
            firsts = range(half * PANELS // HALVES, (half + 1) * PANELS // HALVES)
            source = jnp.concatenate([source_in[q] for q in firsts], axis=1)
            found = found + nn((source - pending).astype(BF16), columns_half(half))
        solved[...] = found

    @pl.when(odd)
    def _():
        columns_near()
        rows_far()
        columns_far()
        arrive(M_FAR, 128, 4)
        arrive(NOISE, 4, 3)

    @pl.when(jnp.logical_or(third, top))
    def _():
        arrive(SOURCE, 4, 15)
        arrive(I_FAR, 128, 4)

    @pl.when(second)
    def _():
        arrive(LOW_UP, 8, 32)
        pending = total(low_up_in, 0, 2 * PANELS)
        cut_parts(nn((sep_source[...] - pending).astype(BF16), sep_inverse[0]), parts_out)
        spread(parts_out, parts_in, 0, SEP_RS, m, True)
        arrive(SEP_RS, 8, 15)
        solved[...] = unfold(total(parts_in, 0, PANELS))

    @pl.when(third)
    def _():
        front_forward(8)

    @pl.when(top)
    def _():
        front_forward(4)

    slot = jnp.where(m == 5, SIDE, 0) + y
    parent = jnp.where(third, 7, 3)

    @pl.when(inner)
    def _():
        front = solved[...].astype(BF16)
        for half in range(HALVES):
            update = nn(front, sep_rows[:, half * HALF : (half + 1) * HALF])
            sep_up_out[half] = fold(update).astype(BF16)
            for q in row:
                copy(sep_up_out.at[half], sep_up_in.at[half, slot], SEP_UP + half, parent, q)

    @pl.when(second)
    def _():
        arrive(I_FAR, 128, 4)

    @pl.when(odd)
    def _():
        noise = jnp.concatenate([wanted_in[k] for k in range(SIDE)], axis=1)
        solved[...] = solved[...] + noise

    @pl.when(even)
    def _():
        solved[...] = jnp.concatenate([wanted_in[k] for k in range(SIDE)], axis=1)

    def mapped_back(into, kind, rows, count):
        found = jnp.zeros((PART, GROUP), F32)
        for half in range(HALVES):
            arrive(kind + half, 16, count)
            view = unfold(total(into.at[half], 0, SIDE)).astype(BF16)
            found = found + nt(view, rows[:, half * HALF : (half + 1) * HALF])
        return found

    @pl.when(jnp.logical_not(top))
    def _():
        solved[...] = solved[...] - mapped_back(down_in, DOWN, sep_rows, SIDE)

    residual = solved[...].astype(BF16)

    @pl.when(odd)
    def _():
        for half in range(HALVES):
            sample = nt(residual, columns_half(half))
            down_out[half] = fold(sample).astype(BF16)
            part = down_out.at[half]

            def descend(leaf):
                for q in row:
                    copy(part, down_in.at[half, y], DOWN + half, leaf, q)

            @pl.when(top)
            def _():
                descend(3)

            @pl.when(third)
            def _():
                descend(1)
                descend(5)

            @pl.when(second)
            def _():
                descend(m + 1)
                descend(m - 1)

            for q in range(PANELS // HALVES):
                out_out[half * PANELS // HALVES + q] = sample[:, q * ROWS : (q + 1) * ROWS]

        spread(out_out, out_in, 0, OUT, m, True)
        arrive(OUT, 4, 15)
        for split in range(SIDE):
            sep_sample[split * PART : (split + 1) * PART, :] = total(out_in, split * SIDE, SIDE)
        arrive(SAMPLE, 8, 16)

    @pl.when(even)
    def _():
        parts_in[p] = fold(solved[...]).astype(BF16)
        for q in others:
            copy(parts_in.at[p], parts_in.at[p], SEP_RES, m, q)
        arrive(SEP_RES, 8, 15)
        sample = nt(joined_parts(parts_in), sep_inverse[0])
        sample_in[p] = sample.astype(BF16)
        for q in others:
            copy(sample_in.at[p], sample_in.at[p], SAMPLE, m, q)
            copy(sample_in.at[p], sample_in.at[p], SAMPLE, m + 1, q)
        copy(sample_in.at[p], sample_in.at[p], SAMPLE, m + 1, p)
        sep_sample[...] = sample
        arrive(SAMPLE, 8, 15)

    correction = nt(joined_columns(sample_in), leaf_rows[...])
    leaf_residual_in[p] = (leaf_solved + leaf_noise[...] - correction).astype(BF16)
    for q in others:
        copy(leaf_residual_in.at[p], leaf_residual_in.at[p], LEAF_RES, m, q)
    arrive(LEAF_RES, 8, 15)
    leaf_sample[...] = nt(joined_columns(leaf_residual_in), leaf_inverse[0])

    sent(LEAF_RS, 8, 15)
    sent(LEAF_RES, 8, 15)
    sent(M_NEAR, 128, 8)
    sent(M_FAR, 128, 4)

    @pl.when(even)
    def _():
        sent(LEAF_UP, 8, 15)
        sent(SEP_RS, 8, 15)
        sent(LOW_UP, 8, 16)
        sent(WANTED, 4, 3)
        sent(SEP_RES, 8, 15)
        sent(SAMPLE, 8, 31)

    @pl.when(odd)
    def _():
        sent(LEAF_UP, 8, 16)
        sent(NOISE, 4, 3)
        sent(I_TURN, 128, 3)
        sent(I_NEAR, 128, 8)
        sent(I_FAR, 128, 4)
        sent(OUT, 4, 15)

    @pl.when(jnp.logical_or(third, top))
    def _():
        sent(SOURCE, 4, 15)

    @pl.when(second)
    def _():
        sent(SEP_RS, 8, 15)

    @pl.when(inner)
    def _():
        for half in range(HALVES):
            sent(SEP_UP + half, 16, 4)
            sent(DOWN + half, 16, 8)

    @pl.when(top)
    def _():
        for half in range(HALVES):
            sent(DOWN + half, 16, 4)


def shards(*arrays):
    vmem = pl.BlockSpec(memory_space=pltpu.VMEM)
    hbm = pl.BlockSpec(memory_space=pl.ANY)
    share = jax.ShapeDtypeStruct((SAMPLES, ROWS), F32)
    vector = pltpu.VMEM((SAMPLES, ROWS), F32)
    block = pltpu.VMEM((1, ROWS, WIDTH), BF16)
    targets = pltpu.VMEM((1, WIDTH), jnp.int32)
    slots = pltpu.VMEM((PANELS, SAMPLES, ROWS), BF16)
    pair = pltpu.VMEM((2 * PANELS, SAMPLES, ROWS), BF16)
    split = pltpu.VMEM((PANELS, 2 * PART, GROUP // 2), BF16)
    rows = pltpu.VMEM((GROUP, WIDTH), BF16)
    partial = (2 * PART, HALF // 2)
    pieces = pltpu.VMEM((PANELS, PART, ROWS), F32)
    ring = pltpu.VMEM((SIDE, PART, ROWS), F32)
    return pl.pallas_call(
        kernel,
        out_shape=(share, share),
        in_specs=[hbm] * 8 + [pl.BlockSpec(memory_space=pltpu.SMEM)] + [hbm] * 2,
        out_specs=(vmem, vmem),
        scratch_shapes=[vector] * 4
        + [block] * 4
        + [targets] * 2
        + [pltpu.SemaphoreType.DMA((10,))]
        + [rows, pltpu.VMEM((ROWS, WIDTH), BF16)]
        + [pltpu.VMEM((SIDE, ROWS, GROUP), BF16), pltpu.VMEM((PANELS, ROWS, GROUP), BF16)]
        + [slots, slots, slots, pair]
        + [slots, slots, slots, pair]
        + [split, split]
        + [pltpu.VMEM((HALVES,) + partial, BF16), pltpu.VMEM((HALVES, 2 * SIDE) + partial, BF16)]
        + [pltpu.VMEM((HALVES,) + partial, BF16), pltpu.VMEM((HALVES, SIDE) + partial, BF16)]
        + [pieces, pieces]
        + [slots, slots]
        + [pieces, vector, ring, pltpu.VMEM((PART, GROUP), F32)]
        + [pltpu.SemaphoreType.DMA((KINDS,)), pltpu.SemaphoreType.DMA((KINDS,))],
        compiler_params=pltpu.CompilerParams(
            collective_id=0, has_side_effects=True, vmem_limit_bytes=60 * 1024 * 1024
        ),
    )(*arrays)


def solution(mesh):
    in_specs = (
        P(None, ("leaf", "panel")),
        P(None, ("leaf", "panel")),
        P(None, ("leaf", "panel")),
        P(None, ("leaf", "panel")),
        P("leaf", "panel", None),
        P("leaf", "panel", None),
        P("leaf", "panel", None),
        P("leaf", "panel", None),
        P("leaf"),
        P("leaf", None),
        P("leaf", None),
    )
    out_specs = (P(None, ("leaf", "panel")), P(None, ("leaf", "panel")))
    return jax.shard_map(shards, mesh=mesh, in_specs=in_specs, out_specs=out_specs, check_vma=False)
```

time: 86.4 us -> 82.5 us (0.955)
  Pallas kernels: 83 us -> 78.9 us
    pallas_call x1, Pallas kernels: 83 us -> 78.9 us  [shards(): pl.pallas_call(kernel, out_shape=(share, share), in_specs=[hbm] * 8 + [pl...]
where the time goes in v5:
time: 82.5 us; the launch traced here: 82.1 us
  Pallas kernels  78.9 us (96%)
  local copies, waits for them, and re-layouts  1.94 us (2%)
  between operations  1.3 us (2%)
    pallas_call x1, Pallas kernels, shards(): pl.pallas_call(kernel, out_shape=(share, share), in_specs=[hbm] * 8 + [pl...  78.9 us
    unnamed x4, local copies, waits for them, and re-layouts  1.94 us

profile of v5, /device:TPU:1, one launch (start us, length us, event | category | flops | bytes accessed | tf_op | source)
XLA Modules:
  0.0 82.1 jit_solution(11102098396213714334)
XLA Ops:
  1.3 78.9 %shard_map.122 = (f32[32,128]{1,0:T(8,128)}, f32[32,128]{1,0:T(8,128)}) custom-call(f32[32,128]{1,0:T(8,128)} %leaf_source_hbm.1, f32[32,128]{1,0:T(8,128)} %leaf_noise_hbm.1, f32[32,128]{1,0:T(8,128)} %sep_source_hbm.1, f32[32,128]{1,0:T(8,128)} %sep_noise_hbm.1, bf16[1,128,2048]{2,1,0:T(8,128)(2,1)} %leaf_inverse_hbm.1, ...), custom_call_target="tpu_custom_call" | custom-call | tf_op jit(solution)/shard_map/pallas_call | solution.py:583
  80.2 0.0 copy-start
  80.2 1.3 %copy.16 = f32[32,128]{1,0:T(8,128)} copy(f32[32,128]{1,0:T(8,128)} %get-tuple-element.4) | data formatting | bytes 32768
  81.5 0.0 copy-done
  81.5 0.6 copy.17
Async XLA Ops:
  80.2 1.3 %copy-start = (f32[32,128]{1,0:T(8,128)S(1)}, f32[32,128]{1,0:T(8,128)}, u32[]{:S(2)}) copy-start(f32[32,128]{1,0:T(8,128)} %get-tuple-element.5) | copy-start | bytes 49156

commit v6 on v5

--- a/solution.py
+++ b/solution.py
@@ -251,8 +251,8 @@
     for load in loads[2:4] + loads[8:]:
         load.wait()
 
-    def rows_near():
-        part = slab(sep_rows, z)
+    def rows_near(first=0, count=ROWS):
+        part = slab(sep_rows, z, first, count)
         for by in (1, 3):
             copy(part, part, M_NEAR, m, zs[by] + y)
 
@@ -336,7 +336,7 @@
     @pl.when(odd)
     def _():
         columns_turn()
-        rows_near()
+        rows_near(0, ROWS // 2)
         for by in (2, 1, 3):
             part = sep_noise.at[pl.ds(pl.multiple_of(step(z, by) * PART, PART), PART)]
             copy(part, wanted_in.at[z], NOISE, m, zs[by] + y)
@@ -360,6 +360,8 @@
     @pl.when(odd)
     def _():
         spread(leaf_up_out, leaf_up_in, PANELS, LEAF_UP, m - 1, False)
+        rows_near(ROWS // 2, ROWS // 2)
+        columns_near()
 
     low_parent = jnp.where(lax.rem(m, 4) == 0, m + 1, m - 1)
     low_slot = jnp.where(lax.rem(m, 4) == 0, 0, PANELS)
@@ -380,10 +382,10 @@
         for by in (2, 1, 3):
             part = wanted_out.at[pl.ds(pl.multiple_of(step(z, by) * PART, PART), PART)]
             copy(part, wanted_in.at[z], WANTED, m, zs[by] + y)
+        arrive(WANTED, 4, 3)
         rows_near()
         rows_far()
         arrive(M_FAR, 128, 4)
-        arrive(WANTED, 4, 3)
 
     def columns_half(half):
         return sep_columns[half * PANELS // HALVES : (half + 1) * PANELS // HALVES].reshape(HALF, GROUP)
@@ -400,14 +402,12 @@
 
     @pl.when(odd)
     def _():
-        columns_near()
         rows_far()
+
+    @pl.when(jnp.logical_or(third, top))
+    def _():
         columns_far()
         arrive(M_FAR, 128, 4)
-        arrive(NOISE, 4, 3)
-
-    @pl.when(jnp.logical_or(third, top))
-    def _():
         arrive(SOURCE, 4, 15)
         arrive(I_FAR, 128, 4)
 
@@ -417,8 +417,10 @@
         pending = total(low_up_in, 0, 2 * PANELS)
         cut_parts(nn((sep_source[...] - pending).astype(BF16), sep_inverse[0]), parts_out)
         spread(parts_out, parts_in, 0, SEP_RS, m, True)
+        columns_far()
         arrive(SEP_RS, 8, 15)
         solved[...] = unfold(total(parts_in, 0, PANELS))
+        arrive(M_FAR, 128, 4)
 
     @pl.when(third)
     def _():
@@ -446,6 +448,7 @@
 
     @pl.when(odd)
     def _():
+        arrive(NOISE, 4, 3)
         noise = jnp.concatenate([wanted_in[k] for k in range(SIDE)], axis=1)
         solved[...] = solved[...] + noise
 

time: 82.5 us -> 77.9 us (0.944)
  Pallas kernels: 78.9 us -> 74.4 us
    pallas_call x1, Pallas kernels: 78.9 us -> 74.4 us  [shards(): pl.pallas_call(kernel, out_shape=(share, share), in_specs=[hbm] * 8 + [pl...]
where the time goes in v6:
time: 77.9 us; the launch traced here: 77.6 us
  Pallas kernels  74.4 us (96%)
  local copies, waits for them, and re-layouts  1.94 us (2%)
  between operations  1.3 us (2%)
    pallas_call x1, Pallas kernels, shards(): pl.pallas_call(kernel, out_shape=(share, share), in_specs=[hbm] * 8 + [pl...  74.4 us
    unnamed x4, local copies, waits for them, and re-layouts  1.94 us

profile of v6, /device:TPU:1, one launch (start us, length us, event | category | flops | bytes accessed | tf_op | source)
XLA Modules:
  0.0 77.6 jit_solution(11063840605853565153)
XLA Ops:
  1.3 74.4 %shard_map.122 = (f32[32,128]{1,0:T(8,128)}, f32[32,128]{1,0:T(8,128)}) custom-call(f32[32,128]{1,0:T(8,128)} %leaf_source_hbm.1, f32[32,128]{1,0:T(8,128)} %leaf_noise_hbm.1, f32[32,128]{1,0:T(8,128)} %sep_source_hbm.1, f32[32,128]{1,0:T(8,128)} %sep_noise_hbm.1, bf16[1,128,2048]{2,1,0:T(8,128)(2,1)} %leaf_inverse_hbm.1, ...), custom_call_target="tpu_custom_call" | custom-call | tf_op jit(solution)/shard_map/pallas_call | solution.py:586
  75.7 0.0 copy-start
  75.7 1.3 %copy.16 = f32[32,128]{1,0:T(8,128)} copy(f32[32,128]{1,0:T(8,128)} %get-tuple-element.4) | data formatting | bytes 32768
  77.0 0.0 copy-done
  77.0 0.6 copy.17
Async XLA Ops:
  75.7 1.3 %copy-start = (f32[32,128]{1,0:T(8,128)S(1)}, f32[32,128]{1,0:T(8,128)}, u32[]{:S(2)}) copy-start(f32[32,128]{1,0:T(8,128)} %get-tuple-element.5) | copy-start | bytes 49156

commit v7 on v6

--- a/solution.py
+++ b/solution.py
@@ -61,11 +61,10 @@
     leaf_coupling_hbm,
     sep_inverse_hbm,
     sep_coupling_hbm,
-    sep_length,
+    sep_length_hbm,
     leaf_map_hbm,
     sep_map_hbm,
-    leaf_sample,
-    sep_sample,
+    samples,
     leaf_source,
     leaf_noise,
     sep_source,
@@ -76,6 +75,7 @@
     sep_coupling,
     leaf_map,
     sep_map,
+    sep_length,
     load_sems,
     sep_rows,
     leaf_rows,
@@ -117,6 +117,7 @@
                 (sep_map_hbm, sep_map),
                 (sep_coupling_hbm, sep_coupling),
                 (sep_inverse_hbm, sep_inverse),
+                (sep_length_hbm, sep_length),
                 (sep_source_hbm, sep_source),
                 (sep_noise_hbm, sep_noise),
                 (leaf_noise_hbm, leaf_noise),
@@ -225,10 +226,12 @@
     for q in range(PANELS):
         leaf_rs_out[q] = leaf_partial[:, q * ROWS : (q + 1) * ROWS].astype(BF16)
     leaf_rs_in[p] = leaf_rs_out[p]
-    def prepare():
-        for load in loads[4:8]:
+    def prepare_rows():
+        for load in loads[4:6]:
             load.wait()
         mapped(sep_coupling, sep_map, slab(sep_rows, z))
+
+    def prepare_inverse():
         length = sep_length[0]
         row_live = lax.broadcasted_iota(jnp.int32, (ROWS, WIDTH), 0) + p * ROWS < length
         column_live = lax.broadcasted_iota(jnp.int32, (ROWS, WIDTH), 1) < length
@@ -240,15 +243,9 @@
 
     @pl.when(odd)
     def _():
-        prepare()
-        for group in range(SIDE):
-            for k in range(SIDE):
-                first = (k * SIDE + group) * ROWS
-                turned[group, :, k * ROWS : (k + 1) * ROWS] = sep_inverse[0, :, first : first + ROWS]
-        sep_columns[p] = turned[y]
-        source_in[p] = mine(sep_source)
-
-    for load in loads[2:4] + loads[8:]:
+        prepare_rows()
+
+    for load in loads[2:4] + loads[6:]:
         load.wait()
 
     def rows_near(first=0, count=ROWS):
@@ -335,6 +332,13 @@
 
     @pl.when(odd)
     def _():
+        prepare_inverse()
+        for group in range(SIDE):
+            for k in range(SIDE):
+                first = (k * SIDE + group) * ROWS
+                turned[group, :, k * ROWS : (k + 1) * ROWS] = sep_inverse[0, :, first : first + ROWS]
+        sep_columns[p] = turned[y]
+        source_in[p] = mine(sep_source)
         columns_turn()
         rows_near(0, ROWS // 2)
         for by in (2, 1, 3):
@@ -368,7 +372,8 @@
 
     @pl.when(even)
     def _():
-        prepare()
+        prepare_rows()
+        prepare_inverse()
         arrive(LEAF_UP, 8, 31)
         pending = total(leaf_up_in, 0, 2 * PANELS)
         cut_columns(nn((sep_source[...] - pending).astype(BF16), sep_inverse[0]), sep_rs_out)
@@ -501,7 +506,7 @@
         spread(out_out, out_in, 0, OUT, m, True)
         arrive(OUT, 4, 15)
         for split in range(SIDE):
-            sep_sample[split * PART : (split + 1) * PART, :] = total(out_in, split * SIDE, SIDE)
+            samples[1, split * PART : (split + 1) * PART, :] = total(out_in, split * SIDE, SIDE)
         arrive(SAMPLE, 8, 16)
 
     @pl.when(even)
@@ -516,7 +521,7 @@
             copy(sample_in.at[p], sample_in.at[p], SAMPLE, m, q)
             copy(sample_in.at[p], sample_in.at[p], SAMPLE, m + 1, q)
         copy(sample_in.at[p], sample_in.at[p], SAMPLE, m + 1, p)
-        sep_sample[...] = sample
+        samples[1] = sample
         arrive(SAMPLE, 8, 15)
 
     correction = nt(joined_columns(sample_in), leaf_rows[...])
@@ -524,7 +529,7 @@
     for q in others:
         copy(leaf_residual_in.at[p], leaf_residual_in.at[p], LEAF_RES, m, q)
     arrive(LEAF_RES, 8, 15)
-    leaf_sample[...] = nt(joined_columns(leaf_residual_in), leaf_inverse[0])
+    samples[0] = nt(joined_columns(leaf_residual_in), leaf_inverse[0])
 
     sent(LEAF_RS, 8, 15)
     sent(LEAF_RES, 8, 15)
@@ -583,15 +588,16 @@
     partial = (2 * PART, HALF // 2)
     pieces = pltpu.VMEM((PANELS, PART, ROWS), F32)
     ring = pltpu.VMEM((SIDE, PART, ROWS), F32)
-    return pl.pallas_call(
+    both = pl.pallas_call(
         kernel,
-        out_shape=(share, share),
-        in_specs=[hbm] * 8 + [pl.BlockSpec(memory_space=pltpu.SMEM)] + [hbm] * 2,
-        out_specs=(vmem, vmem),
+        out_shape=jax.ShapeDtypeStruct((2, SAMPLES, ROWS), F32),
+        in_specs=[hbm] * 11,
+        out_specs=vmem,
         scratch_shapes=[vector] * 4
         + [block] * 4
         + [targets] * 2
-        + [pltpu.SemaphoreType.DMA((10,))]
+        + [pltpu.SMEM((1,), jnp.int32)]
+        + [pltpu.SemaphoreType.DMA((11,))]
         + [rows, pltpu.VMEM((ROWS, WIDTH), BF16)]
         + [pltpu.VMEM((SIDE, ROWS, GROUP), BF16), pltpu.VMEM((PANELS, ROWS, GROUP), BF16)]
         + [slots, slots, slots, pair]
@@ -607,6 +613,7 @@
             collective_id=0, has_side_effects=True, vmem_limit_bytes=60 * 1024 * 1024
         ),
     )(*arrays)
+    return both[0], both[1]
 
 
 def solution(mesh):

time: 77.9 us -> 77.2 us (level)
    unnamed x4 -> x0, local copies, waits for them, and re-layouts: 1.94 us -> none
    squeeze x0 -> x1, local copies, waits for them, and re-layouts: none -> 1.35 us  [shards(): return (both[0], both[1])]
where the time goes in v7:
time: 77.2 us; the launch traced here: 76.9 us
  Pallas kernels  74.3 us (96%)
  local copies, waits for them, and re-layouts  1.35 us (2%)
  between operations  1.29 us (2%)
    pallas_call x1, Pallas kernels, shards(): pl.pallas_call(kernel, out_shape=jax.ShapeDtypeStruct((2, SAMPLES, ROWS),...  74.3 us

profile of v7, /device:TPU:1, one launch (start us, length us, event | category | flops | bytes accessed | tf_op | source)
XLA Modules:
  0.0 76.9 jit_solution(4380597164666624332)
XLA Ops:
  1.3 74.3 %shard_map.122 = f32[2,32,128]{2,1,0:T(8,128)} custom-call(f32[32,128]{1,0:T(8,128)} %leaf_source_hbm.1, f32[32,128]{1,0:T(8,128)} %leaf_noise_hbm.1, f32[32,128]{1,0:T(8,128)} %sep_source_hbm.1, f32[32,128]{1,0:T(8,128)} %sep_noise_hbm.1, bf16[1,128,2048]{2,1,0:T(8,128)(2,1)} %leaf_inverse_hbm.1, bf16[1,128,2048]{2,1,0:T(8,128)(2,1)} %leaf_coupling_hbm.1, ...), custom_call_target="tpu_custom_call" | custom-call | tf_op jit(solution)/shard_map/pallas_call | solution.py:591
  75.5 1.3 %slice_bitcast_fusion = (f32[32,128]{1,0:T(8,128)}, f32[32,128]{1,0:T(8,128)}) fusion(f32[2,32,128]{2,1,0:T(8,128)} %shard_map.122), kind=kLoop, calls=%fused_computation | loop fusion | bytes 65536 | tf_op jit(solution)/shard_map/squeeze | solution.py:616

commit v8 on v7

--- a/solution.py
+++ b/solution.py
@@ -241,10 +241,6 @@
     def mine(value_ref):
         return value_ref[pl.ds(pl.multiple_of(z * PART, PART), PART), :]
 
-    @pl.when(odd)
-    def _():
-        prepare_rows()
-
     for load in loads[2:4] + loads[6:]:
         load.wait()
 
@@ -340,7 +336,6 @@
         sep_columns[p] = turned[y]
         source_in[p] = mine(sep_source)
         columns_turn()
-        rows_near(0, ROWS // 2)
         for by in (2, 1, 3):
             part = sep_noise.at[pl.ds(pl.multiple_of(step(z, by) * PART, PART), PART)]
             copy(part, wanted_in.at[z], NOISE, m, zs[by] + y)
@@ -353,6 +348,11 @@
             copy(part, source_in.at[p], SOURCE, m, zs[dz] + ys[dy])
 
     mapped(leaf_coupling, leaf_map, leaf_rows)
+
+    @pl.when(odd)
+    def _():
+        prepare_rows()
+
     arrive(LEAF_RS, 8, 15)
     leaf_solved = total(leaf_rs_in, 0, PANELS)
     cut_columns(nn(leaf_solved.astype(BF16), leaf_rows[...]), leaf_up_out)
@@ -364,7 +364,7 @@
     @pl.when(odd)
     def _():
         spread(leaf_up_out, leaf_up_in, PANELS, LEAF_UP, m - 1, False)
-        rows_near(ROWS // 2, ROWS // 2)
+        rows_near()
         columns_near()
 
     low_parent = jnp.where(lax.rem(m, 4) == 0, m + 1, m - 1)

time: 77.2 us -> 83.8 us (1.085)
  Pallas kernels: 74.3 us -> 80.9 us
    pallas_call x1, Pallas kernels: 74.3 us -> 80.9 us  [shards(): pl.pallas_call(kernel, out_shape=jax.ShapeDtypeStruct((2, SAMPLES, ROWS),...]
where the time goes in v8:
time: 83.8 us; the launch traced here: 83.5 us
  Pallas kernels  80.9 us (97%)
  local copies, waits for them, and re-layouts  1.35 us (2%)
  between operations  1.29 us (2%)
    pallas_call x1, Pallas kernels, shards(): pl.pallas_call(kernel, out_shape=jax.ShapeDtypeStruct((2, SAMPLES, ROWS),...  80.9 us

profile of v8, /device:TPU:1, one launch (start us, length us, event | category | flops | bytes accessed | tf_op | source)
XLA Modules:
  0.0 83.5 jit_solution(2404791143684754657)
XLA Ops:
  1.3 80.9 %shard_map.122 = f32[2,32,128]{2,1,0:T(8,128)} custom-call(f32[32,128]{1,0:T(8,128)} %leaf_source_hbm.1, f32[32,128]{1,0:T(8,128)} %leaf_noise_hbm.1, f32[32,128]{1,0:T(8,128)} %sep_source_hbm.1, f32[32,128]{1,0:T(8,128)} %sep_noise_hbm.1, bf16[1,128,2048]{2,1,0:T(8,128)(2,1)} %leaf_inverse_hbm.1, bf16[1,128,2048]{2,1,0:T(8,128)(2,1)} %leaf_coupling_hbm.1, ...), custom_call_target="tpu_custom_call" | custom-call | tf_op jit(solution)/shard_map/pallas_call | solution.py:591
  82.1 1.3 %slice_bitcast_fusion = (f32[32,128]{1,0:T(8,128)}, f32[32,128]{1,0:T(8,128)}) fusion(f32[2,32,128]{2,1,0:T(8,128)} %shard_map.122), kind=kLoop, calls=%fused_computation | loop fusion | bytes 65536 | tf_op jit(solution)/shard_map/squeeze | solution.py:616
